TPU v7x, 256 devices: a whole 4x4x8 slice. The times are simulated.
256 devices in a mesh: dp: 8 (over z), ctx: 32 (over x, y, core).
Axes of the slice: x: 4, y: 4, z: 8, core: 2. Of those that a mesh axis runs over, the one named last changes fastest.
Arguments:
- query_vectors: bfloat16 [8, 4096, 2048], P('dp', 'ctx'), may hold values from -6 to 6
- key_vectors: bfloat16 [8, 4096, 2048], P('dp', 'ctx'), may hold values from -6 to 6
- value_vectors: bfloat16 [8, 4096, 2048], P('dp', 'ctx'), may hold values from -13 to 13
- output_grad: bfloat16 [8, 4096, 2048], P('dp', 'ctx'), may hold values from -39 to 39
- feature_weight: bfloat16 [2048, 128], replicated, may hold values from -0.5 to 0.5
Outputs:
- attended: bfloat16 [8, 4096, 2048], P('dp', 'ctx')
- query_grad: bfloat16 [8, 4096, 2048], P('dp', 'ctx')
- key_grad: bfloat16 [8, 4096, 2048], P('dp', 'ctx')
- value_grad: bfloat16 [8, 4096, 2048], P('dp', 'ctx')
- weight_grad: float32 [2048, 128], P('ctx')
All inputs are finite; a program needn't handle non-finite values.
Results may differ from a plain program's by a relative error of at most 0.0085.
The roundings to bfloat16 on the way count: a program that leaves them out, or rounds other values in their place, can miss the bound.
Values sent between devices are 32-bit elements; how exact they have to be, the bound alone decides.
A program may use at most 192 MiB of HBM per device.

v0:
```python
import jax
import jax.numpy as jnp
from jax import lax
from jax.sharding import PartitionSpec as P

HEAD = 128


epsilon = 1e-05
highest = lax.Precision.HIGHEST


def prefix_2(value, axis, join, neutral, backward):
    count, mine = (lax.axis_size(axis), lax.axis_index(axis))
    pieces = lax.all_gather(value, axis)
    if backward:
        pieces = pieces[::-1]
        mine = count - 1 - mine
    running = jnp.full_like(value, 0) + jnp.asarray(neutral, value.dtype)

    def turn(position, running):
        longer = join(running, pieces[position])
        return jnp.where(position < mine, longer, running)

    return lax.fori_loop(0, count - 1, turn, running)


def feature_map(activation):
    return jax.nn.elu(activation) + 1.0


def feature_slope(activation):
    return jnp.where(activation > 0.0, 1.0, jnp.exp(jnp.minimum(activation, 0.0)))


def product(pattern, former, latter):
    return jnp.einsum(pattern, former, latter, preferred_element_type=jnp.float32)


def exact_product(pattern, former, latter):
    return jnp.einsum(
        pattern, former.astype(jnp.float32), latter.astype(jnp.float32), precision=highest
    )


def add_states(earlier, later):
    return earlier + later


def body(query_vectors, key_vectors, value_vectors, output_grad, feature_weight):
    seq_count, tok_count, row_width = query_vectors.shape
    feat_count = feature_weight.shape[1]
    head_count = row_width // HEAD
    block_shape = (seq_count, tok_count, head_count, HEAD)
    weights = feature_weight.reshape(head_count, HEAD, feat_count)
    query_blk = query_vectors.reshape(block_shape)
    key_blk = key_vectors.reshape(block_shape)
    value_blk = value_vectors.reshape(block_shape)
    grad_blk = output_grad.reshape(block_shape).astype(jnp.float32)
    query_pre = product("bthe,hef->bthf", query_blk, weights)
    key_pre = product("bthe,hef->bthf", key_blk, weights)
    query_feat = feature_map(query_pre).astype(jnp.bfloat16)
    key_feat = feature_map(key_pre).astype(jnp.bfloat16)
    local_state = product("bthf,bthe->bhfe", key_feat, value_blk)
    prefix = prefix_2(local_state, "ctx", add_states, jnp.zeros_like(local_state), False)
    positions = jnp.arange(tok_count)
    causal = positions[:, None] >= positions[None, :]
    scores = product("bthf,buhf->bhtu", query_feat, key_feat)
    score_low = jnp.where(causal, scores, 0.0).astype(jnp.bfloat16)
    numerator = exact_product("bthf,bhfe->bthe", query_feat, prefix) + product(
        "bhtu,buhe->bthe", score_low, value_blk
    )
    scale_inv = lax.rsqrt(jnp.mean(numerator * numerator, axis=-1, keepdims=True) + epsilon)
    normed = numerator * scale_inv
    attended = normed.astype(jnp.bfloat16)
    grad_numer = (
        scale_inv * (grad_blk - normed * jnp.mean(grad_blk * normed, axis=-1, keepdims=True))
    ).astype(jnp.bfloat16)
    back_scores = jnp.where(causal, product("bthe,buhe->bhtu", grad_numer, value_blk), 0.0).astype(
        jnp.bfloat16
    )
    local_grad = product("bthf,bthe->bhfe", query_feat, grad_numer)
    suffix = prefix_2(local_grad, "ctx", add_states, jnp.zeros_like(local_grad), True)
    query_feat_grad = exact_product("bhfe,bthe->bthf", prefix, grad_numer) + product(
        "bhtu,buhf->bthf", back_scores, key_feat
    )
    key_feat_grad = exact_product("bhfe,bthe->bthf", suffix, value_blk) + product(
        "bhtu,bthf->buhf", back_scores, query_feat
    )
    value_grad = exact_product("bhfe,bthf->bthe", suffix, key_feat) + product(
        "bhtu,bthe->buhe", score_low, grad_numer
    )
    query_pre_grad = (query_feat_grad * feature_slope(query_pre)).astype(jnp.bfloat16)
    key_pre_grad = (key_feat_grad * feature_slope(key_pre)).astype(jnp.bfloat16)
    query_grad = product("bthf,hef->bthe", query_pre_grad, weights)
    key_grad = product("bthf,hef->bthe", key_pre_grad, weights)
    weight_local = product("bthe,bthf->hef", query_blk, query_pre_grad) + product(
        "bthe,bthf->hef", key_blk, key_pre_grad
    )
    weight_local = weight_local.reshape(row_width, feat_count)
    grand_total = lax.psum(weight_local, ("dp", "ctx"))
    share_rows = row_width // lax.axis_size("ctx")
    weight_grad = lax.dynamic_slice_in_dim(
        grand_total, lax.axis_index("ctx") * share_rows, share_rows, 0
    )
    flat_shape = (seq_count, tok_count, row_width)
    return (
        attended.reshape(flat_shape),
        query_grad.astype(jnp.bfloat16).reshape(flat_shape),
        key_grad.astype(jnp.bfloat16).reshape(flat_shape),
        value_grad.astype(jnp.bfloat16).reshape(flat_shape),
        weight_grad,
    )


def solution(mesh):
    in_specs = (
        P("dp", "ctx", None),
        P("dp", "ctx", None),
        P("dp", "ctx", None),
        P("dp", "ctx", None),
        P(),
    )
    out_specs = (
        P("dp", "ctx", None),
        P("dp", "ctx", None),
        P("dp", "ctx", None),
        P("dp", "ctx", None),
        P("ctx", None),
    )
    return jax.shard_map(body, mesh=mesh, in_specs=in_specs, out_specs=out_specs, check_vma=False)
```

profile of v0, /device:TPU:2, one launch (start us, length us, event | category | flops | bytes accessed | tf_op | source)
XLA Modules:
  0.0 656.9 jit_solution(721301000422096765)
XLA Ops:
  15.1 2.4 copy.52
  20.4 115.1 %all-gather.5.cloned.1.call-done = f32[512,128,128]{2,1,0:T(8,128)} async-done(((f32[16,128,128]{2,1,0:T(8,128)}), f32[512,128,128]{2,1,0:T(8,128)}) %all-gather.5.cloned.1.call-update) | async-done | bytes 33554448 | tf_op jit(solution)/shard_map/all_gather | solution.py:15
  135.6 50.0 %while.28 = (s32[]{:T(128)}, f32[1,16,128,128]{3,2,1,0:T(8,128)S(1)}, s32[]{:T(128)}, f32[32,1,16,128,128]{4,3,2,1,0:T(8,128)}, s32[]{:T(128)}, /*index=5*/s32[]{:T(128)}) while((s32[]{:T(128)}, f32[1,16,128,128]{3,2,1,0:T(8,128)S(1)}, s32[]{:T(128)}, f32[32,1,16,128,128]{4,3,2,1,0:T(8,128)}, s32[]{:T(128)}, ...), condition=%wide.region_1.2_spmd.clone, body=%wide.region_0.1_spmd.clone.sunk | while | flops 786436 | bytes 3145821 | solution.py:25
  137.2 1.6 add_select_fusion.4
  138.8 1.6 add_select_fusion.4
  140.4 1.6 add_select_fusion.4
  142.0 1.6 add_select_fusion.4
  143.6 1.6 add_select_fusion.4
  145.2 1.6 add_select_fusion.4
  146.8 1.6 add_select_fusion.4
  148.5 1.6 add_select_fusion.4
  150.1 1.6 add_select_fusion.4
  151.7 1.6 add_select_fusion.4
  153.3 1.6 add_select_fusion.4
  156.5 1.6 add_select_fusion.4
  158.1 1.6 add_select_fusion.4
  159.8 1.6 add_select_fusion.4
  161.4 1.6 add_select_fusion.4
  164.6 1.6 add_select_fusion.4
  166.2 1.6 add_select_fusion.4
  167.8 1.6 add_select_fusion.4
  172.7 1.6 add_select_fusion.4
  174.3 1.6 add_select_fusion.4
  175.9 1.6 add_select_fusion.4
  180.7 1.6 add_select_fusion.4
  182.3 1.6 add_select_fusion.4
  184.0 1.6 add_select_fusion.4
  189.6 2.3 fusion.25
  194.4 1.7 convolution_bitcast_fusion.8
  196.1 1.7 fusion.10
  197.8 1.9 fusion.12
  200.8 2.0 copy.69
  202.9 2.0 copy.68
  204.9 2.6 fusion.34
  207.5 105.0 %all-gather.7.cloned.1.call-done = f32[512,128,128]{2,1,0:T(8,128)} async-done(((f32[16,128,128]{2,1,0:T(8,128)}), f32[512,128,128]{2,1,0:T(8,128)}) %all-gather.7.cloned.1.call-update) | async-done | bytes 33554448 | tf_op jit(solution)/shard_map/all_gather | solution.py:15
  312.5 23.1 %rev.3 = f32[32,1,16,128,128]{4,3,2,1,0:T(8,128)} reverse(f32[32,1,16,128,128]{4,3,2,1,0:T(8,128)} %bitcast.157), dimensions={0} | reverse | bytes 67108864 | tf_op jit(solution)/shard_map/rev | solution.py:17
  335.6 50.0 %while.29 = (s32[]{:T(128)}, f32[1,16,128,128]{3,2,1,0:T(8,128)S(1)}, s32[]{:T(128)}, f32[32,1,16,128,128]{4,3,2,1,0:T(8,128)}, s32[]{:T(128)}, /*index=5*/s32[]{:T(128)}) while((s32[]{:T(128)}, f32[1,16,128,128]{3,2,1,0:T(8,128)S(1)}, s32[]{:T(128)}, f32[32,1,16,128,128]{4,3,2,1,0:T(8,128)}, s32[]{:T(128)}, ...), condition=%wide.region_5.6_spmd.clone, body=%wide.region_4.5_spmd.clone.sunk | while | flops 786436 | bytes 3145821 | solution.py:25
  337.2 1.6 add_select_fusion.5
  338.8 1.6 add_select_fusion.5
  340.4 1.6 add_select_fusion.5
  342.1 1.6 add_select_fusion.5
  343.7 1.6 add_select_fusion.5
  345.3 1.6 add_select_fusion.5
  346.9 1.6 add_select_fusion.5
  350.1 1.6 add_select_fusion.5
  353.4 1.6 add_select_fusion.5
  356.6 1.6 add_select_fusion.5
  359.8 1.6 add_select_fusion.5
  363.0 1.6 add_select_fusion.5
  366.3 1.6 add_select_fusion.5
  367.9 1.6 add_select_fusion.5
  369.5 1.6 add_select_fusion.5
  371.1 1.6 add_select_fusion.5
  372.7 1.6 add_select_fusion.5
  374.3 1.6 add_select_fusion.5
  376.0 1.6 add_select_fusion.5
  377.6 1.6 add_select_fusion.5
  380.8 1.6 add_select_fusion.5
  384.0 1.6 add_select_fusion.5
  386.8 2.0 convolution_bitcast_fusion.6
  388.8 1.8 fusion.13
  390.7 2.9 convolution_add_fusion
  393.6 1.8 fusion.11
  397.7 251.3 %all-reduce.2.cloned.1.call-done = f32[2048,128]{1,0:T(8,128)} async-done(((f32[2048,128]{1,0:T(8,128)}), f32[2048,128]{1,0:T(8,128)}) %all-reduce.2.cloned.1.call-update) | async-done | bytes 1048592 | tf_op jit(solution)/shard_map/psum | solution.py:101
  (68 shorter events, 48.7 us)
Async XLA Ops:
  7.2 1.4 copy-start
  7.2 128.4 %all-gather.5.cloned.1.call-start = ((), (), s32[]{:S(2)}) async-start(), calls=%async_computation.1 | async-start | bytes 34603008 | tf_op jit(solution)/shard_map/all_gather | solution.py:15
  8.6 0.8 copy-start.8
  9.8 1.0 copy-start.3
  12.3 181.8 %copy-start.5 = (bf16[16,8,16,128]{3,2,1,0:T(8,128)(2,1)}, bf16[16,8,16,128]{3,2,1,0:T(8,128)(2,1)S(1)}, u32[]{:S(2)}) copy-start(bf16[16,8,16,128]{3,2,1,0:T(8,128)(2,1)S(1)} %copy.90) | copy-start | bytes 1572868
  13.7 298.9 %all-gather.7.cloned.1.call-start = ((), (), s32[]{:S(2)}) async-start(), calls=%async_computation.2 | async-start | bytes 34603008 | tf_op jit(solution)/shard_map/all_gather | solution.py:15
  15.0 2.4 copy-start.9
  17.8 1.0 copy-start.4
  19.3 174.9 %copy-start.1 = (bf16[128,16,128]{0,2,1:T(8,128)(2,1)}, bf16[128,16,128]{0,2,1:T(8,128)(2,1)S(1)}, u32[]{:S(2)}) copy-start(bf16[128,16,128]{0,2,1:T(8,128)(2,1)S(1)} %fusion.26) | copy-start | bytes 1572868
  191.9 0.8 copy-start.7
  194.2 454.8 %all-reduce.2.cloned.1.call-start = ((), (), s32[]{:S(2)}) async-start(), calls=%async_computation | async-start | bytes 2097152 | tf_op jit(solution)/shard_map/psum | solution.py:101
  197.8 114.7 %copy-start.10 = (bf16[16,128,128]{2,1,0:T(8,128)(2,1)}, bf16[16,128,128]{2,1,0:T(8,128)(2,1)S(1)}, u32[]{:S(2)}) copy-start(bf16[16,128,128]{2,1,0:T(8,128)(2,1)S(1)} %fusion.10) | copy-start | bytes 1572868
  312.5 73.1 %copy-start.6 = (bf16[16,8,16,128]{3,2,1,0:T(8,128)(2,1)S(1)}, bf16[16,8,16,128]{3,2,1,0:T(8,128)(2,1)}, u32[]{:S(2)}) copy-start(bf16[16,8,16,128]{3,2,1,0:T(8,128)(2,1)} %copy-done.5) | copy-start | bytes 1572868
  312.5 76.3 %copy-start.2 = (bf16[128,16,128]{0,2,1:T(8,128)(2,1)S(1)}, bf16[128,16,128]{0,2,1:T(8,128)(2,1)}, u32[]{:S(2)}) copy-start(bf16[128,16,128]{0,2,1:T(8,128)(2,1)} %copy-done.1) | copy-start | bytes 1572868
Sparse Core Ops, SparseCore 0:
  13.8 121.7 all-gather.4
  194.3 118.1 all-gather.6
  393.7 255.3 all-reduce.1
where the time goes:
time: 660 us; the launch traced here: 657 us
  waiting for transfers between devices  472 us (72%)
  other arithmetic  103 us (16%)
  local copies, waits for them, and re-layouts  40.3 us (6%)
  matrix products  26.1 us (4%)
  between operations  14 us (2%)
    psum x1, waiting for transfers between devices, body(): grand_total = lax.psum(weight_local, ('dp', 'ctx'))  251 us
    all_gather x2, waiting for transfers between devices, prefix_2(): pieces = lax.all_gather(value, axis)  220 us
    select_n x62, other arithmetic, turn(): return jnp.where(position < mine, longer, running)  98.5 us
    rev x1, local copies, waits for them, and re-layouts, prefix_2(): pieces = pieces[::-1]  23.1 us
    dot_general x14, matrix products, product(): jnp.einsum(pattern, former, latter, preferred_element_type=jnp.float32)  20.3 us
  transfers between devices with their start and end apart: 3, of which 3 were waited for; matrix products, arithmetic and copies ran while one was open for 3% of the time, Pallas kernels for 0%

commit v1 on v0

v1 whole, which is shorter than its diff:
```python
import functools

import jax
import jax.numpy as jnp
from jax import lax
from jax.experimental import pallas as pl
from jax.experimental.pallas import tpu as pltpu
from jax.sharding import PartitionSpec as P

HEAD = 128
EPS = 1e-05
MESH = pl.DeviceIdType.MESH
BF = jnp.bfloat16
F32 = jnp.float32


def dot(a, b, ca, cb):
    return lax.dot_general(a, b, (((ca,), (cb,)), ((), ())), preferred_element_type=F32)


def split(x):
    high = x.astype(BF)
    return high, (x - high.astype(F32)).astype(BF)


def kernel(
    n_dp, n_chip, heads, groups, tok,
    q_hbm, k_hbm, v_hbm, g_hbm, w_hbm,
    att_hbm, dq_hbm, dk_hbm, dv_hbm, wg_hbm,
    q_ref, k_ref, v_ref, g_ref, w_ref,
    att_ref, dq_ref, dk_ref, dv_ref, wg_ref,
    qf_ref, kf_ref, sq_ref, sk_ref, sc_ref, nl_ref, m_ref, dkl_ref, dvl_ref,
    state, sib, pair, gat, pre, ret, oth, sib2,
    wl_ref, wsib, wpair, wgat, zsrc, zgat, zsum,
    in_sem, w_sem, out_sem,
    s_sib, r_sib, s_gat, r_gat, s_ret, r_ret, s_sib2, r_sib2,
    s_ws, r_ws, s_wg, r_wg, s_z1, r_z1, s_z2, r_z2,
):
    dp = lax.axis_index("dp")
    ctx = lax.axis_index("ctx")
    chip, core = lax.div(ctx, 2), lax.rem(ctx, 2)
    sibling = ctx + 1 - 2 * core
    per = heads // groups
    half = per // 2
    rows = half * HEAD
    piece = rows // n_chip
    hw = HEAD // 2

    def peer(d):
        other = lax.rem(chip + d, n_chip)
        return other, other * 2 + core

    def remote(src, dst, ssem, rsem, device):
        return pltpu.make_async_remote_copy(
            src_ref=src, dst_ref=dst, send_sem=ssem, recv_sem=rsem,
            device_id=device, device_id_type=MESH,
        )

    def cols(h, n=1):
        return pl.ds(pl.multiple_of(h * HEAD, HEAD), n * HEAD)

    loads = []
    w_load = pltpu.make_async_copy(w_hbm, w_ref, w_sem)
    w_load.start()
    for g in range(groups):
        cs = pl.ds(g * per * HEAD, per * HEAD)
        mine = []
        for i, (src, dst) in enumerate(
            ((k_hbm, k_ref), (q_hbm, q_ref), (v_hbm, v_ref), (g_hbm, g_ref))
        ):
            c = pltpu.make_async_copy(src.at[0, :, cs], dst.at[:, cs], in_sem.at[g, i])
            c.start()
            mine.append(c)
        loads.append(mine)

    barrier = pltpu.get_barrier_semaphore()

    def greet(device):
        pl.semaphore_signal(barrier, inc=1, device_id=device, device_id_type=MESH)

    greet((dp, sibling))

    @pl.loop(1, n_chip)
    def _(d):
        greet((dp, peer(d)[1]))

    @pl.loop(1, n_dp)
    def _(d):
        greet((lax.rem(dp + d, n_dp), ctx))

    rowid = lax.broadcasted_iota(jnp.int32, (tok, tok), 0)
    colid = lax.broadcasted_iota(jnp.int32, (tok, tok), 1)
    causal = rowid >= colid

    def phi(z):
        return jnp.where(z > 0.0, z + 1.0, jnp.exp(jnp.minimum(z, 0.0)))

    def each(g, body):
        @pl.loop(g * per // 2, (g + 1) * per // 2)
        def _(i):
            body(2 * i)
            body(2 * i + 1)

    def forward_state(h):
        c = cols(h)
        z = dot(k_ref[:, c], w_ref[c, :], 1, 0)
        f = phi(z)
        kf = f.astype(BF)
        kf_ref[:, c] = kf
        sk_ref[:, c] = jnp.minimum(f, 1.0)
        state[0, c, :] = dot(kf, v_ref[:, c], 0, 0)

    def forward_local(h):
        c = cols(h)
        z = dot(q_ref[:, c], w_ref[c, :], 1, 0)
        f = phi(z)
        qf = f.astype(BF)
        qf_ref[:, c] = qf
        sq_ref[:, c] = jnp.minimum(f, 1.0)
        w = jnp.where(causal, dot(qf, kf_ref[:, c], 1, 1), 0.0).astype(BF)
        sc_ref[:, c] = w
        nl_ref[:, c] = dot(w, v_ref[:, c], 1, 0)

    def numer(h):
        c = cols(h)
        qf = qf_ref[:, c]
        ph, plo = split(state[0, c, :])
        n = dot(qf, ph, 1, 0) + dot(qf, plo, 1, 0) + nl_ref[:, c]
        r = lax.rsqrt(jnp.mean(n * n, axis=-1, keepdims=True) + EPS)
        normed = n * r
        att_ref[:, c] = normed.astype(BF)
        og = g_ref[:, c].astype(F32)
        m = (r * (og - normed * jnp.mean(og * normed, axis=-1, keepdims=True))).astype(BF)
        m_ref[:, c] = m
        state[1, c, :] = dot(qf, m, 0, 0)

    def back_local(h):
        c = cols(h)
        m, qf, kf = m_ref[:, c], qf_ref[:, c], kf_ref[:, c]
        ph, plo = split(state[0, c, :])
        b = jnp.where(causal, dot(m, v_ref[:, c], 1, 1), 0.0).astype(BF)
        qg = dot(m, ph, 1, 1) + dot(m, plo, 1, 1) + dot(b, kf, 1, 0)
        qp = (qg * sq_ref[:, c]).astype(BF)
        dq_ref[:, c] = dot(qp, w_ref[c, :], 1, 1).astype(BF)
        wl_ref[c, :] = dot(q_ref[:, c], qp, 0, 0)
        dkl_ref[:, c] = dot(b, qf, 0, 0)
        dvl_ref[:, c] = dot(sc_ref[:, c], m, 0, 0)

    def back_final(h):
        c = cols(h)
        qh, ql = split(state[1, c, :])
        v, kf = v_ref[:, c], kf_ref[:, c]
        kg = dot(v, qh, 1, 1) + dot(v, ql, 1, 1) + dkl_ref[:, c]
        kp = (kg * sk_ref[:, c]).astype(BF)
        dk_ref[:, c] = dot(kp, w_ref[c, :], 1, 1).astype(BF)
        dv_ref[:, c] = (dot(kf, qh, 1, 0) + dot(kf, ql, 1, 0) + dvl_ref[:, c]).astype(BF)
        wl_ref[c, :] += dot(k_ref[:, c], kp, 0, 0)

    def mine_rows(g):
        return pl.ds(pl.multiple_of((g * per + core * half) * HEAD, HEAD), rows)

    def other_rows(g):
        return pl.ds(pl.multiple_of((g * per + (1 - core) * half) * HEAD, HEAD), rows)

    def scan_sib(e, g):
        remote(
            state.at[e, other_rows(g), :], sib.at[e, g], s_sib.at[e, g], r_sib.at[e, g],
            (dp, sibling),
        ).start()

    def own_piece():
        return pl.ds(pl.multiple_of(chip * piece, piece), piece)

    def scan_gather(e, g):
        remote(
            sib.at[e, g], sib.at[e, g], s_sib.at[e, g], r_sib.at[e, g], (dp, sibling)
        ).wait_recv()
        pair[e, g] = state[e, mine_rows(g), :] + sib[e, g]

        @pl.loop(1, n_chip)
        def _(d):
            other, device = peer(d)
            remote(
                pair.at[e, g, pl.ds(pl.multiple_of(other * piece, piece), piece), :],
                gat.at[e, g, chip], s_gat.at[e, g], r_gat.at[e, g], (dp, device),
            ).start()

        gat[e, g, chip] = pair[e, g, own_piece(), :]

    def bulk(buf, ssem, rsem):
        return remote(buf, buf, ssem, rsem, (dp, sibling))

    def scan_return(e, g):
        bulk(gat.at[e, g, pl.ds(0, n_chip - 1)], s_gat.at[e, g], r_gat.at[e, g]).wait_recv()
        order = range(n_chip) if e == 0 else range(n_chip - 1, -1, -1)
        total = jnp.zeros((piece, HEAD), F32)
        for p in order:
            pre[e, g, p] = total
            total = total + gat[e, g, p]

        @pl.loop(1, n_chip)
        def _(d):
            other, device = peer(d)
            remote(
                pre.at[e, g, other], ret.at[e, g, own_piece(), :],
                s_ret.at[e, g], r_ret.at[e, g], (dp, device),
            ).start()

        ret[e, g, own_piece(), :] = pre[e, g, chip]

    def scan_share(e, g):
        span = (n_chip - 1) * piece
        bulk(ret.at[e, g, pl.ds(0, span), :], s_ret.at[e, g], r_ret.at[e, g]).wait_recv()
        base = ret[e, g]
        local = state[e, mine_rows(g), :]
        near = sib[e, g]
        give = (core == 0) if e == 0 else (core == 1)
        oth[e, g] = base + jnp.where(give, local, 0.0)
        remote(
            oth.at[e, g], sib2.at[e, g], s_sib2.at[e, g], r_sib2.at[e, g], (dp, sibling)
        ).start()
        state[e, mine_rows(g), :] = base + jnp.where(give, 0.0, near)

    def scan_done(e, g):
        bulk(sib.at[e, g], s_sib.at[e, g], r_sib.at[e, g]).wait_send()
        bulk(sib2.at[e, g], s_sib2.at[e, g], r_sib2.at[e, g]).wait_recv()
        state[e, other_rows(g), :] = sib2[e, g]

    def head_half(h, c):
        return pl.ds(pl.multiple_of(h * HEAD + c * hw, hw), hw)

    def weight_sib(g):
        for i in range(per):
            wpair[1, g, i] = wl_ref[head_half(g * per + i, 1 - core), :]
        remote(wpair.at[1, g], wsib.at[g], s_ws.at[g], r_ws.at[g], (dp, sibling)).start()

    def weight_gather(g):
        bulk(wsib.at[g], s_ws.at[g], r_ws.at[g]).wait_recv()
        for i in range(per):
            h = g * per + i
            wpair[0, g, i] = wl_ref[head_half(h, core), :] + wsib[g, i]

            @pl.when(chip != h)
            def _():
                remote(
                    wpair.at[0, g, i], wgat.at[chip], s_wg.at[g], r_wg, (dp, 2 * h + core)
                ).start()

            @pl.when(chip == h)
            def _():
                wgat[chip] = wpair[0, g, i]

    def weight_finish():
        bulk(wgat.at[pl.ds(0, n_chip - 1)], s_wg.at[0], r_wg).wait_recv()
        total = wgat[0]
        for p in range(1, n_chip):
            total = total + wgat[p]
        zsrc[...] = total.reshape(n_dp, hw // n_dp, HEAD)

        @pl.loop(1, n_dp)
        def _(d):
            other = lax.rem(dp + d, n_dp)
            remote(zsrc.at[other], zgat.at[dp], s_z1, r_z1, (other, ctx)).start()

        zgat[dp] = zsrc[dp]
        bulk(zgat.at[pl.ds(0, n_dp - 1)], s_z1, r_z1).wait_recv()
        total = zgat[0]
        for z in range(1, n_dp):
            total = total + zgat[z]
        zsum[...] = total

        @pl.loop(1, n_dp)
        def _(d):
            other = lax.rem(dp + d, n_dp)
            remote(zsum, wg_ref.at[dp], s_z2, r_z2, (other, ctx)).start()

        wg_ref[dp] = total
        bulk(wg_ref.at[pl.ds(0, n_dp - 1)], s_z2, r_z2).wait_recv()

    stores = []

    def store(i, g, src, dst):
        cs = pl.ds(g * per * HEAD, per * HEAD)
        c = pltpu.make_async_copy(src.at[:, cs], dst.at[0, :, cs], out_sem.at[i, g])
        c.start()
        stores.append(c)

    G = range(groups)
    w_load.wait()
    for g in G:
        loads[g][0].wait()
        loads[g][2].wait()
        each(g, forward_state)
        if g == 0:
            pl.semaphore_wait(barrier, 1 + (n_chip - 1) + (n_dp - 1))
        scan_sib(0, g)
    for g in G:
        scan_gather(0, g)
    for g in G:
        loads[g][1].wait()
        each(g, forward_local)
    for g in G:
        scan_return(0, g)
    for g in G:
        scan_share(0, g)
    for g in G:
        scan_done(0, g)
        loads[g][3].wait()
        each(g, numer)
        store(0, g, att_ref, att_hbm)
        scan_sib(1, g)
    for g in G:
        scan_gather(1, g)
    each(0, back_local)
    for g in G:
        scan_return(1, g)
    for g in range(1, groups):
        each(g, back_local)
    for g in G:
        store(1, g, dq_ref, dq_hbm)
    for g in G:
        scan_share(1, g)
    for g in G:
        scan_done(1, g)
        each(g, back_final)
        weight_sib(g)
        store(2, g, dk_ref, dk_hbm)
        store(3, g, dv_ref, dv_hbm)
    for g in G:
        weight_gather(g)
    weight_finish()
    wg_out = pltpu.make_async_copy(wg_ref, wg_hbm, w_sem)
    wg_out.start()

    for g in G:
        for e in range(2):
            bulk(gat.at[e, g, pl.ds(0, n_chip - 1)], s_gat.at[e, g], r_gat.at[e, g]).wait_send()
            bulk(pre.at[e, g, pl.ds(0, n_chip - 1)], s_ret.at[e, g], r_ret.at[e, g]).wait_send()
            bulk(oth.at[e, g], s_sib2.at[e, g], r_sib2.at[e, g]).wait_send()
        bulk(wsib.at[g], s_ws.at[g], r_ws.at[g]).wait_send()
        inside = (chip >= g * per) & (chip < (g + 1) * per)

        @pl.when(inside)
        def _():
            bulk(wpair.at[0, g, pl.ds(0, per - 1)], s_wg.at[g], r_wg).wait_send()

        @pl.when(jnp.logical_not(inside))
        def _():
            bulk(wpair.at[0, g], s_wg.at[g], r_wg).wait_send()

    bulk(zsrc.at[pl.ds(0, n_dp - 1)], s_z1, r_z1).wait_send()
    bulk(wg_ref.at[pl.ds(0, n_dp - 1)], s_z2, r_z2).wait_send()
    for c in stores:
        c.wait()
    wg_out.wait()


def body(n_dp, n_ctx, groups, q, k, v, g, w):
    _, tok, width = q.shape
    heads = width // HEAD
    n_chip = n_ctx // 2
    per = heads // groups
    rows = per // 2 * HEAD
    piece = rows // n_chip
    hw = HEAD // 2
    act = pltpu.VMEM((tok, width), BF)
    wide = pltpu.VMEM((tok, width), F32)
    dma = pltpu.SemaphoreType.DMA
    block = pltpu.VMEM((2, groups, rows, HEAD), F32)
    slots = pltpu.VMEM((2, groups, n_chip, piece, HEAD), F32)
    scratch = (
        [act] * 4 + [pltpu.VMEM((width, HEAD), BF)]
        + [act] * 4 + [pltpu.VMEM((n_dp, hw // n_dp, HEAD), F32)]
        + [act, act, wide, wide, act, wide, act, wide, wide]
        + [pltpu.VMEM((2, width, HEAD), F32), block, block, slots, slots, block, block, block]
        + [
            pltpu.VMEM((width, HEAD), F32),
            pltpu.VMEM((groups, per, hw, HEAD), F32),
            pltpu.VMEM((2, groups, per, hw, HEAD), F32),
            pltpu.VMEM((n_chip, hw, HEAD), F32),
            pltpu.VMEM((n_dp, hw // n_dp, HEAD), F32),
            pltpu.VMEM((n_dp, hw // n_dp, HEAD), F32),
            pltpu.VMEM((hw // n_dp, HEAD), F32),
        ]
        + [dma((groups, 4)), dma, dma((4, groups))]
        + [dma((2, groups))] * 8
        + [dma((groups,))] * 3 + [dma] * 5
    )
    out = jax.ShapeDtypeStruct(q.shape, BF)
    hbm = pl.BlockSpec(memory_space=pl.ANY)
    att, dq, dk, dv, wg = pl.pallas_call(
        functools.partial(kernel, n_dp, n_chip, heads, groups, tok),
        out_shape=[out] * 4 + [jax.ShapeDtypeStruct((n_dp, hw // n_dp, HEAD), F32)],
        in_specs=[hbm] * 5,
        out_specs=[hbm] * 5,
        scratch_shapes=scratch,
        compiler_params=pltpu.CompilerParams(
            collective_id=0, has_side_effects=True, vmem_limit_bytes=48 * 1024 * 1024
        ),
        cost_estimate=pl.CostEstimate(
            flops=40 * heads * HEAD**3, bytes_accessed=5 * 2**20, transcendentals=0
        ),
    )(q, k, v, g, w)
    return att, dq, dk, dv, wg.reshape(hw, HEAD)


def solution(mesh):
    n_dp, n_ctx = mesh.shape["dp"], mesh.shape["ctx"]
    spec = P("dp", "ctx", None)
    return jax.shard_map(
        functools.partial(body, n_dp, n_ctx, 2),
        mesh=mesh,
        in_specs=(spec, spec, spec, spec, P()),
        out_specs=(spec, spec, spec, spec, P("ctx", None)),
        check_vma=False,
    )
```

time: 660 us -> 83.7 us (0.13)
  the two profiles are of different devices: /device:TPU:2 before, /device:TPU:6 now
where the time goes in v1:
time: 83.7 us; the launch traced here: 83.4 us
  Pallas kernels  73.7 us (88%)
  local copies, waits for them, and re-layouts  8.99 us (11%)
    pallas_call x1, Pallas kernels, body(): pl.pallas_call(functools.partial(kernel, n_dp, n_chip, heads, groups, tok...  73.7 us
    unnamed x15, local copies, waits for them, and re-layouts  8.99 us

profile of v1, /device:TPU:6, one launch (start us, length us, event | category | flops | bytes accessed | tf_op | source)
XLA Modules:
  0.0 83.4 jit_solution(707492503598459739)
XLA Ops:
  0.6 0.0 copy-start
  0.6 1.0 %copy-done = bf16[1,128,2048]{2,1,0:T(8,128)(2,1)S(1)} copy-done((bf16[1,128,2048]{2,1,0:T(8,128)(2,1)S(1)}, bf16[1,128,2048]{2,1,0:T(8,128)(2,1)}, u32[]{:S(2)}) %copy-start) | copy-done | bytes 524312
  1.7 0.0 copy-start.1
  1.7 1.0 %copy-done.1 = bf16[1,128,2048]{2,1,0:T(8,128)(2,1)S(1)} copy-done((bf16[1,128,2048]{2,1,0:T(8,128)(2,1)S(1)}, bf16[1,128,2048]{2,1,0:T(8,128)(2,1)}, u32[]{:S(2)}) %copy-start.1) | copy-done | bytes 524312
  2.7 0.0 copy-start.2
  2.7 1.0 %copy-done.2 = bf16[1,128,2048]{2,1,0:T(8,128)(2,1)S(1)} copy-done((bf16[1,128,2048]{2,1,0:T(8,128)(2,1)S(1)}, bf16[1,128,2048]{2,1,0:T(8,128)(2,1)}, u32[]{:S(2)}) %copy-start.2) | copy-done | bytes 524312
  3.8 0.0 copy-start.3
  3.8 1.0 %copy-done.3 = bf16[1,128,2048]{2,1,0:T(8,128)(2,1)S(1)} copy-done((bf16[1,128,2048]{2,1,0:T(8,128)(2,1)S(1)}, bf16[1,128,2048]{2,1,0:T(8,128)(2,1)}, u32[]{:S(2)}) %copy-start.3) | copy-done | bytes 524312
  4.8 0.0 copy-start.4
  4.8 1.0 %copy-done.4 = bf16[2048,128]{1,0:T(8,128)(2,1)S(1)} copy-done((bf16[2048,128]{1,0:T(8,128)(2,1)S(1)}, bf16[2048,128]{1,0:T(8,128)(2,1)}, u32[]{:S(2)}) %copy-start.4) | copy-done | bytes 524312
  5.8 73.7 %shard_map.92 = (bf16[1,128,2048]{2,1,0:T(8,128)(2,1)S(1)}, bf16[1,128,2048]{2,1,0:T(8,128)(2,1)S(1)}, bf16[1,128,2048]{2,1,0:T(8,128)(2,1)S(1)}, bf16[1,128,2048]{2,1,0:T(8,128)(2,1)S(1)}, f32[8,8,128]{2,1,0:T(8,128)S(1)}) custom-call(bf16[1,128,2048]{2,1,0:T(8,128)(2,1)S(1)} %copy-done, bf16[1,128,2048]{2,1,0:T(8,128)(2,1)S(1)} %copy-done.1, ...), custom_call_target="tpu_custom_call" | custom-call | flops 1342177280 | bytes 5242880 | tf_op jit(solution)/shard_map/pallas_call | solution.py:391
  79.6 0.8 copy.15
  80.4 0.8 copy.16
  81.2 0.8 copy.17
  82.0 0.8 copy.18
  82.8 0.6 copy.19
Async XLA Ops:
  0.6 1.0 %copy-start = (bf16[1,128,2048]{2,1,0:T(8,128)(2,1)S(1)}, bf16[1,128,2048]{2,1,0:T(8,128)(2,1)}, u32[]{:S(2)}) copy-start(bf16[1,128,2048]{2,1,0:T(8,128)(2,1)} %q_hbm.1) | copy-start | bytes 1572868
  1.7 1.0 %copy-start.1 = (bf16[1,128,2048]{2,1,0:T(8,128)(2,1)S(1)}, bf16[1,128,2048]{2,1,0:T(8,128)(2,1)}, u32[]{:S(2)}) copy-start(bf16[1,128,2048]{2,1,0:T(8,128)(2,1)} %k_hbm.1) | copy-start | bytes 1572868
  2.7 1.0 %copy-start.2 = (bf16[1,128,2048]{2,1,0:T(8,128)(2,1)S(1)}, bf16[1,128,2048]{2,1,0:T(8,128)(2,1)}, u32[]{:S(2)}) copy-start(bf16[1,128,2048]{2,1,0:T(8,128)(2,1)} %v_hbm.1) | copy-start | bytes 1572868
  3.8 1.0 %copy-start.3 = (bf16[1,128,2048]{2,1,0:T(8,128)(2,1)S(1)}, bf16[1,128,2048]{2,1,0:T(8,128)(2,1)}, u32[]{:S(2)}) copy-start(bf16[1,128,2048]{2,1,0:T(8,128)(2,1)} %g_hbm.1) | copy-start | bytes 1572868
  4.8 1.0 %copy-start.4 = (bf16[2048,128]{1,0:T(8,128)(2,1)S(1)}, bf16[2048,128]{1,0:T(8,128)(2,1)}, u32[]{:S(2)}) copy-start(bf16[2048,128]{1,0:T(8,128)(2,1)} %w_hbm.1) | copy-start | bytes 1572868

commit v2 on v1

v2 whole, which is shorter than its diff:
```python
import functools

import jax
import jax.numpy as jnp
from jax import lax
from jax.experimental import pallas as pl
from jax.experimental.pallas import tpu as pltpu
from jax.sharding import PartitionSpec as P

HEAD = 128
ORDER = (
    "fs0", "fs1", "fs2", "fs3", "b00", "b01", "b02", "b03", "fl0", "fl1", "fl2", "fl3", "c00",
    "c01", "c02", "c03", "e00", "e01", "nu0", "e02", "nu1", "b10", "e03", "nu2", "b11", "nu3",
    "b12", "bl0", "b13", "bl1", "bl2", "c10", "bl3", "c11", "c12", "c13", "e10", "e11", "bf0",
    "e12", "bf1", "wb0", "e13", "bf2", "wb1", "bf3", "wb2", "wb3",
)
EPS = 1e-05
SIDE = 4
PER = 4
FAR_FIRST = sorted(
    [(x, y) for x in range(SIDE) for y in range(SIDE) if x or y],
    key=lambda d: -sum(min(s, SIDE - s) for s in d),
)
MESH = pl.DeviceIdType.MESH
BF = jnp.bfloat16
F32 = jnp.float32


def dot(a, b, ca, cb):
    return lax.dot_general(a, b, (((ca,), (cb,)), ((), ())), preferred_element_type=F32)


def split(x):
    high = x.astype(BF)
    return high, (x - high.astype(F32)).astype(BF)


def phi(z):
    return jnp.where(z > 0.0, z + 1.0, jnp.exp(jnp.minimum(z, 0.0)))


def write_out(*refs):
    src, dst, mid, sems = refs[:5], refs[5:10], refs[10:15], refs[15]
    ins = [pltpu.make_async_copy(src[i], mid[i], sems.at[0, i]) for i in range(5)]
    outs = [pltpu.make_async_copy(mid[i], dst[i], sems.at[1, i]) for i in range(5)]
    for c in ins:
        c.start()
    for a, b in zip(ins, outs):
        a.wait()
        b.start()
    for c in outs:
        c.wait()


def kernel(
    n_dp, heads, tok,
    q_hbm, k_hbm, v_hbm, g_hbm, w_hbm,
    att_hbm, dq_hbm, dk_hbm, dv_hbm, wg_hbm,
    q_ref, k_ref, v_ref, g_ref, w_ref,
    att_ref, dq_ref, dk_ref, dv_ref, wg_ref,
    qf_ref, kf_ref, sq_ref, sk_ref, sct_ref, nl_ref, m_ref, dkl_ref, dvl_ref,
    state, full, sib, pair, ygat, pre, ret, oth,
    wl_ref, wsib, wpair, wgat, zsrc, zgat,
    in_sem, w_sem, out_sem,
    s_sib, r_sib, s_y, r_y, s_ret, r_ret, s_sib2, r_sib2,
    s_ws, r_ws, s_wg, r_wg, s_z, r_z, near_sem, far_sem,
):
    dp = lax.axis_index("dp")
    ctx = lax.axis_index("ctx")
    core = lax.rem(ctx, 2)
    chip = lax.div(ctx, 2)
    cx, cy = lax.div(chip, SIDE), lax.rem(chip, SIDE)
    sibling = ctx + 1 - 2 * core
    groups = heads // PER
    rows = PER // 2 * HEAD
    piece = rows // (SIDE * SIDE)
    hw = HEAD // 2
    n_chip = SIDE * SIDE

    def plane(dx, dy):
        o = lax.rem(cx + dx, SIDE) * SIDE + lax.rem(cy + dy, SIDE)
        return o, (dp, o * 2 + core)

    def zline(d):
        return (lax.rem(dp + d, n_dp), ctx)

    near = (dp, sibling)

    def remote(src, dst, ssem, rsem, where):
        return pltpu.make_async_remote_copy(
            src_ref=src, dst_ref=dst, send_sem=ssem, recv_sem=rsem,
            device_id=where, device_id_type=MESH,
        )

    def bulk(buf, ssem, rsem):
        return remote(buf, buf, ssem, rsem, near)

    def members(g):
        turn, first = divmod(g * PER, SIDE)
        return [SIDE * i + (i + turn) % SIDE for i in range(first, first + PER)]

    def cols(h):
        return pl.ds(h * HEAD, HEAD)

    def place(g, i):
        return pl.ds((g * PER + i) * HEAD, HEAD)

    w_load = pltpu.make_async_copy(w_hbm, w_ref, w_sem)
    w_load.start()
    loads = []
    for i, (src, dst) in enumerate(
        ((k_hbm, k_ref), (v_hbm, v_ref), (q_hbm, q_ref), (g_hbm, g_ref))
    ):
        loads.append(pltpu.make_async_copy(src.at[0], dst, in_sem.at[i]))
    loads[0].start()
    loads[1].start()

    barrier = pltpu.get_barrier_semaphore()

    def greet(sem, where):
        pl.semaphore_signal(sem, inc=1, device_id=where, device_id_type=MESH)

    greet(barrier, near)
    for d in FAR_FIRST:
        greet(barrier, plane(*d)[1])
    greet(barrier, zline(1))
    greet(barrier, zline(n_dp - 1))

    def enter():
        loads[2].start()
        loads[3].start()
        pl.semaphore_wait(barrier, 1 + len(FAR_FIRST) + 2)
        greet(near_sem, zline(1))
        greet(near_sem, zline(n_dp - 1))

    def relay():
        pl.semaphore_wait(near_sem, 2)
        greet(far_sem, zline(2))
        greet(far_sem, zline(n_dp - 2))

    def relayed():
        pl.semaphore_wait(far_sem, 2)

    rowid = lax.broadcasted_iota(jnp.int32, (tok, tok), 0)
    colid = lax.broadcasted_iota(jnp.int32, (tok, tok), 1)
    causal = rowid >= colid
    causal_t = rowid <= colid

    def lockstep(g, body):
        running = [body(g, i, h) for i, h in enumerate(members(g))]
        while running:
            alive = []
            for r in running:
                try:
                    next(r)
                    alive.append(r)
                except StopIteration:
                    pass
            running = alive

    def forward_state(g, i, h):
        c = cols(h)
        z = dot(k_ref[:, c], w_ref[c, :], 1, 0)
        yield
        f = phi(z)
        kf = f.astype(BF)
        kf_ref[:, c] = kf
        sk_ref[:, c] = jnp.minimum(f, 1.0)
        yield
        state[0, place(g, i), :] = dot(kf, v_ref[:, c], 0, 0)

    def forward_local(g, i, h):
        c = cols(h)
        z = dot(q_ref[:, c], w_ref[c, :], 1, 0)
        yield
        f = phi(z)
        qf = f.astype(BF)
        qf_ref[:, c] = qf
        sq_ref[:, c] = jnp.minimum(f, 1.0)
        yield
        kf = kf_ref[:, c]
        w = jnp.where(causal, dot(qf, kf, 1, 1), 0.0).astype(BF)
        sct_ref[:, c] = jnp.where(causal_t, dot(kf, qf, 1, 1), 0.0).astype(BF)
        yield
        nl_ref[:, c] = dot(w, v_ref[:, c], 1, 0)

    def numer(g, i, h):
        c = cols(h)
        qf = qf_ref[:, c]
        ph, plo = split(full[0, place(g, i), :])
        yield
        n = dot(qf, ph, 1, 0) + dot(qf, plo, 1, 0) + nl_ref[:, c]
        yield
        r = lax.rsqrt(jnp.mean(n * n, axis=-1, keepdims=True) + EPS)
        yield
        normed = n * r
        att_ref[:, c] = normed.astype(BF)
        og = g_ref[:, c].astype(F32)
        s = jnp.mean(og * normed, axis=-1, keepdims=True)
        yield
        m = (r * (og - normed * s)).astype(BF)
        m_ref[:, c] = m
        yield
        state[1, place(g, i), :] = dot(qf, m, 0, 0)

    def back_local(g, i, h):
        c = cols(h)
        m, qf, kf, v = m_ref[:, c], qf_ref[:, c], kf_ref[:, c], v_ref[:, c]
        ph, plo = split(full[0, place(g, i), :])
        b = jnp.where(causal, dot(m, v, 1, 1), 0.0).astype(BF)
        bt = jnp.where(causal_t, dot(v, m, 1, 1), 0.0).astype(BF)
        yield
        qg = dot(m, ph, 1, 1) + dot(m, plo, 1, 1) + dot(b, kf, 1, 0)
        dkl_ref[:, c] = dot(bt, qf, 1, 0)
        dvl_ref[:, c] = dot(sct_ref[:, c], m, 1, 0)
        yield
        qp = (qg * sq_ref[:, c]).astype(BF)
        yield
        dq_ref[:, c] = dot(qp, w_ref[c, :], 1, 1).astype(BF)
        wl_ref[place(g, i), :] = dot(q_ref[:, c], qp, 0, 0)

    def back_final(g, i, h):
        c = cols(h)
        qh, ql = split(full[1, place(g, i), :])
        v, kf = v_ref[:, c], kf_ref[:, c]
        yield
        kg = dot(v, qh, 1, 1) + dot(v, ql, 1, 1) + dkl_ref[:, c]
        dv_ref[:, c] = (dot(kf, qh, 1, 0) + dot(kf, ql, 1, 0) + dvl_ref[:, c]).astype(BF)
        yield
        kp = (kg * sk_ref[:, c]).astype(BF)
        yield
        dk_ref[:, c] = dot(kp, w_ref[c, :], 1, 1).astype(BF)
        wl_ref[place(g, i), :] += dot(k_ref[:, c], kp, 0, 0)

    def half_rows(g, c):
        return pl.ds(pl.multiple_of(g * PER * HEAD + c * rows, rows), rows)

    def part(o):
        return pl.ds(pl.multiple_of(o * piece, piece), piece)

    def scan_a(e, g):
        remote(
            state.at[e, half_rows(g, 1 - core), :], sib.at[e, g],
            s_sib.at[e, g], r_sib.at[e, g], near,
        ).start()

    def scan_b(e, g):
        bulk(sib.at[e, g], s_sib.at[e, g], r_sib.at[e, g]).wait_recv()
        pair[e, g] = state[e, half_rows(g, core), :] + sib[e, g]
        for d in FAR_FIRST:
            o, where = plane(*d)
            remote(
                pair.at[e, g, part(o), :], ygat.at[e, g, chip],
                s_y.at[e, g], r_y.at[e, g], where,
            ).start()
        ygat[e, g, chip] = pair[e, g, part(chip), :]

    def scan_c(e, g):
        bulk(ygat.at[e, g, pl.ds(0, n_chip - 1)], s_y.at[e, g], r_y.at[e, g]).wait_recv()
        order = range(n_chip) if e == 0 else range(n_chip - 1, -1, -1)
        total = jnp.zeros((piece, HEAD), F32)
        for p in order:
            pre[e, g, p] = total
            total = total + ygat[e, g, p]
        for d in FAR_FIRST:
            o, where = plane(*d)
            remote(
                pre.at[e, g, o], ret.at[e, g, part(chip), :],
                s_ret.at[e, g], r_ret.at[e, g], where,
            ).start()
        ret[e, g, part(chip), :] = pre[e, g, chip]

    def scan_e(e, g):
        bulk(
            ret.at[e, g, pl.ds(0, rows - piece), :], s_ret.at[e, g], r_ret.at[e, g]
        ).wait_recv()
        base = ret[e, g]
        local = state[e, half_rows(g, core), :]
        give = core == e
        oth[e, g] = base + jnp.where(give, local, 0.0)
        remote(
            oth.at[e, g], full.at[e, half_rows(g, core), :],
            s_sib2.at[e, g], r_sib2.at[e, g], near,
        ).start()
        full[e, half_rows(g, core), :] = base + jnp.where(give, 0.0, sib[e, g])

    def scan_f(e, g):
        bulk(sib.at[e, g], s_sib2.at[e, g], r_sib2.at[e, g]).wait_recv()

    def weight_a(g):
        for i in range(PER):
            wpair[1, g, i] = wl_ref[
                pl.ds(pl.multiple_of((g * PER + i) * HEAD + (1 - core) * hw, hw), hw), :
            ]
        remote(wpair.at[1, g], wsib.at[g], s_ws.at[g], r_ws.at[g], near).start()

    def weight_b(g):
        bulk(wsib.at[g], s_ws.at[g], r_ws.at[g]).wait_recv()
        for i, h in enumerate(members(g)):
            wpair[0, g, i] = (
                wl_ref[pl.ds(pl.multiple_of((g * PER + i) * HEAD + core * hw, hw), hw), :]
                + wsib[g, i]
            )
        for i, h in enumerate(members(g)):

            @pl.when(chip != h)
            def _():
                remote(
                    wpair.at[0, g, i], wgat.at[chip], s_wg.at[g, i], r_wg, (dp, 2 * h + core)
                ).start()

            @pl.when(chip == h)
            def _():
                wgat[chip] = wpair[0, g, i]

    def weight_c():
        bulk(wgat.at[pl.ds(0, n_chip - 1)], s_z, r_wg).wait_recv()
        total = wgat[0]
        for p in range(1, n_chip):
            total = total + wgat[p]
        zsrc[...] = total
        for d in (4, 3, 5, 2, 6, 1, 7):
            remote(zsrc, zgat.at[dp], s_z, r_z, zline(d)).start()
        zgat[dp] = total
        bulk(zgat.at[pl.ds(0, n_dp - 1)], s_z, r_z).wait_recv()
        total = zgat[0]
        for z in range(1, n_dp):
            total = total + zgat[z]
        wg_ref[...] = total

    stores = []

    def store(i, src, dst):
        c = pltpu.make_async_copy(src, dst.at[0], out_sem.at[i])
        c.start()
        stores.append(c)

    def fs(g):
        lockstep(g, forward_state)
        if g == 0:
            enter()
        scan_a(0, g)

    def fl(g):
        lockstep(g, forward_local)

    def nu(g):
        scan_f(0, g)
        lockstep(g, numer)
        scan_a(1, g)

    def bl(g):
        lockstep(g, back_local)

    def bf(g):
        scan_f(1, g)
        lockstep(g, back_final)
        weight_a(g)

    first = [False] * 4

    def once(i, action):
        if not first[i]:
            first[i] = True
            action()

    def step(word):
        name, g = word[:-1], int(word[-1])
        if name == "fl":
            once(0, lambda: (loads[2].wait(), relay()))
            fl(g)
        elif name == "nu":
            once(1, lambda: (loads[3].wait(), relayed()))
            nu(g)
        elif name in ("fs", "bl", "bf", "wb"):
            {"fs": fs, "bl": bl, "bf": bf, "wb": weight_b}[name](g)
        else:
            {"b": scan_b, "c": scan_c, "e": scan_e}[name[0]](int(name[1]), g)

    w_load.wait()
    loads[0].wait()
    loads[1].wait()
    left = list(ORDER)
    while left:
        step(left.pop(0))
        names = [w[:-1] for w in left]
        if "nu" not in names:
            once(2, lambda: store(0, att_ref, att_hbm))
        if "bl" not in names:
            once(3, lambda: store(1, dq_ref, dq_hbm))
        if names and names[0] == "wb" and "bf" not in names and len(stores) == 2:
            store(2, dk_ref, dk_hbm)
            store(3, dv_ref, dv_hbm)
    weight_c()
    wg_out = pltpu.make_async_copy(wg_ref, wg_hbm, w_sem)
    wg_out.start()

    for g in range(groups):
        for e in range(2):
            bulk(ygat.at[e, g, pl.ds(0, n_chip - 1)], s_y.at[e, g], r_y.at[e, g]).wait_send()
            bulk(pre.at[e, g, pl.ds(0, n_chip - 1)], s_ret.at[e, g], r_ret.at[e, g]).wait_send()
            bulk(sib.at[e, g], s_sib.at[e, g], r_sib.at[e, g]).wait_send()
            bulk(oth.at[e, g], s_sib2.at[e, g], r_sib2.at[e, g]).wait_send()
        bulk(wsib.at[g], s_ws.at[g], r_ws.at[g]).wait_send()
        for i, h in enumerate(members(g)):

            @pl.when(chip != h)
            def _():
                bulk(wpair.at[0, g, i], s_wg.at[g, i], r_wg).wait_send()

    bulk(zgat.at[pl.ds(0, n_dp - 1)], s_z, r_z).wait_send()
    for c in stores:
        c.wait()
    wg_out.wait()


def body(n_dp, q, k, v, g, w):
    _, tok, width = q.shape
    heads = width // HEAD
    groups = heads // PER
    rows = PER // 2 * HEAD
    piece = rows // (SIDE * SIDE)
    hw = HEAD // 2
    act = pltpu.VMEM((tok, width), BF)
    wide = pltpu.VMEM((tok, width), F32)
    dma = pltpu.SemaphoreType.DMA
    block = pltpu.VMEM((2, groups, rows, HEAD), F32)
    slots = pltpu.VMEM((2, groups, SIDE * SIDE, piece, HEAD), F32)
    scratch = (
        [act] * 4 + [pltpu.VMEM((width, HEAD), BF)]
        + [act] * 4 + [pltpu.VMEM((hw, HEAD), F32)]
        + [act, act, wide, wide, act, wide, act, wide, wide]
        + [pltpu.VMEM((2, width, HEAD), F32)] * 2
        + [block, block, slots, slots, block, block]
        + [
            pltpu.VMEM((width, HEAD), F32),
            pltpu.VMEM((groups, PER, hw, HEAD), F32),
            pltpu.VMEM((2, groups, PER, hw, HEAD), F32),
            pltpu.VMEM((SIDE * SIDE, hw, HEAD), F32),
            pltpu.VMEM((hw, HEAD), F32),
            pltpu.VMEM((n_dp, hw, HEAD), F32),
        ]
        + [dma((4,)), dma, dma((4,))]
        + [dma((2, groups))] * 8
        + [dma((groups,))] * 2 + [dma((groups, PER)), dma, dma, dma]
        + [pltpu.SemaphoreType.REGULAR] * 2
    )
    outs = [jax.ShapeDtypeStruct(q.shape, BF)] * 4 + [jax.ShapeDtypeStruct((hw, HEAD), F32)]
    hbm = pl.BlockSpec(memory_space=pl.ANY)
    limit = 63 * 1024 * 1024
    results = pl.pallas_call(
        functools.partial(kernel, n_dp, heads, tok),
        out_shape=outs,
        in_specs=[hbm] * 5,
        out_specs=[hbm] * 5,
        scratch_shapes=scratch,
        compiler_params=pltpu.CompilerParams(
            collective_id=0, has_side_effects=True, vmem_limit_bytes=limit
        ),
        cost_estimate=pl.CostEstimate(
            flops=40 * heads * HEAD**3, bytes_accessed=5 * 2**20, transcendentals=0
        ),
    )(q, k, v, g, w)
    return pl.pallas_call(
        write_out,
        out_shape=outs,
        in_specs=[hbm] * 5,
        out_specs=[hbm] * 5,
        scratch_shapes=[pltpu.VMEM(o.shape, o.dtype) for o in outs] + [dma((2, 5))],
        compiler_params=pltpu.CompilerParams(vmem_limit_bytes=limit),
    )(*results)


def solution(mesh):
    spec = P("dp", "ctx", None)
    return jax.shard_map(
        functools.partial(body, mesh.shape["dp"]),
        mesh=mesh,
        in_specs=(spec, spec, spec, spec, P()),
        out_specs=(spec, spec, spec, spec, P("ctx", None)),
        check_vma=False,
    )
```

time: 83.7 us -> 63.2 us (0.76)
  the two profiles are of different devices: /device:TPU:6 before, /device:TPU:2 now
where the time goes in v2:
time: 63.2 us; the launch traced here: 63 us
  Pallas kernels  62.3 us (99%)
  between operations  0.64 us (1%)
    pallas_call x1, Pallas kernels, body(): pl.pallas_call(functools.partial(kernel, n_dp, heads, tok), out_shape=out...  59.9 us
    pallas_call x1, Pallas kernels, body(): pl.pallas_call(write_out, out_shape=outs, in_specs=[hbm] * 5, out_specs=[...  2.44 us

profile of v2, /device:TPU:2, one launch (start us, length us, event | category | flops | bytes accessed | tf_op | source)
XLA Modules:
  0.0 63.0 jit_solution(6792937681168560060)
XLA Ops:
  0.6 59.9 %shard_map.92 = (bf16[1,128,2048]{2,1,0:T(8,128)(2,1)}, bf16[1,128,2048]{2,1,0:T(8,128)(2,1)}, bf16[1,128,2048]{2,1,0:T(8,128)(2,1)}, bf16[1,128,2048]{2,1,0:T(8,128)(2,1)}, f32[64,128]{1,0:T(8,128)}) custom-call(bf16[1,128,2048]{2,1,0:T(8,128)(2,1)} %q_hbm.1, bf16[1,128,2048]{2,1,0:T(8,128)(2,1)} %k_hbm.1, bf16[1,128,2048]{2,1,0:T(8,128)(2,1)} %v_hbm.1, ...), custom_call_target="tpu_custom_call" | custom-call | flops 1342177280 | bytes 5242880 | tf_op jit(solution)/shard_map/pallas_call | solution.py:451
  60.5 2.4 %shard_map.93 = (bf16[1,128,2048]{2,1,0:T(8,128)(2,1)}, bf16[1,128,2048]{2,1,0:T(8,128)(2,1)}, bf16[1,128,2048]{2,1,0:T(8,128)(2,1)}, bf16[1,128,2048]{2,1,0:T(8,128)(2,1)}, f32[64,128]{1,0:T(8,128)}) custom-call(bf16[1,128,2048]{2,1,0:T(8,128)(2,1)} %get-tuple-element.10.refs_0_, bf16[1,128,2048]{2,1,0:T(8,128)(2,1)} %get-tuple-element.11.refs_1_, ...), custom_call_target="tpu_custom_call" | custom-call | tf_op jit(solution)/shard_map/pallas_call | solution.py:464

commit v3 on v2

v3 whole, which is shorter than its diff:
```python
import functools

import jax
import jax.numpy as jnp
from jax import lax
from jax.experimental import pallas as pl
from jax.experimental.pallas import tpu as pltpu
from jax.sharding import PartitionSpec as P

HEAD = 128
ORDER = (
    "pk0", "pk1", "fs0", "pk2", "fs1", "pk3", "fs2", "fs3", "pq0", "pq1", "pq2", "pq3", "fl0",
    "fl1", "c00", "c01", "fl2", "c02", "fl3", "c03", "relay", "nu0", "nu1", "nu2", "nu3",
    "relayed", "bl0", "bl1", "c10", "bl2", "c11", "bl3", "c12", "c13", "bf0", "bf1", "bf2",
    "bf3",
)
EPS = 1e-05
SIDE = 4
GROUPS = 4
PER = 2
FAR_FIRST = sorted(
    [(x, y) for x in range(SIDE) for y in range(SIDE) if x or y],
    key=lambda d: -sum(min(s, SIDE - s) for s in d),
)
MESH = pl.DeviceIdType.MESH
BF = jnp.bfloat16
F32 = jnp.float32
K, V, Q, G = range(4)
ATT, DQ, DK, DV = range(4)


def dot(a, b, ca, cb):
    return lax.dot_general(a, b, (((ca,), (cb,)), ((), ())), preferred_element_type=F32)


def split(x):
    high = x.astype(BF)
    return high, (x - high.astype(F32)).astype(BF)


def phi(z):
    return jnp.where(z > 0.0, z + 1.0, jnp.exp(jnp.minimum(z, 0.0)))


def write_out(*refs):
    src, dst, mid, sems = refs[:5], refs[5:10], refs[10:15], refs[15]
    ins = [pltpu.make_async_copy(src[i], mid[i], sems.at[0, i]) for i in range(5)]
    outs = [pltpu.make_async_copy(mid[i], dst[i], sems.at[1, i]) for i in range(5)]
    for c in ins:
        c.start()
    for a, b in zip(ins, outs):
        a.wait()
        b.start()
    for c in outs:
        c.wait()


def kernel(
    n_dp, tok,
    q_hbm, k_hbm, v_hbm, g_hbm, w_hbm,
    att_hbm, dq_hbm, dk_hbm, dv_hbm, wg_hbm,
    raw, w_ref, res, wg_ref,
    loc, give, got, back, came,
    qf_ref, kf_ref, sct_ref, m_ref, sq_ref, sk_ref, nl_ref, dkl_ref, dvl_ref,
    state, pair, gat, pre, ret,
    wl_ref, wgat, zsrc, zgat,
    in_sem, w_sem, out_sem,
    s_in, r_in, s_back, r_back, s_gat, r_gat, s_ret, r_ret,
    s_wg, r_wg, s_z, r_z, near_sem, far_sem,
):
    dp = lax.axis_index("dp")
    ctx = lax.axis_index("ctx")
    core = lax.rem(ctx, 2)
    chip = lax.div(ctx, 2)
    cx, cy = lax.div(chip, SIDE), lax.rem(chip, SIDE)
    near = (dp, ctx + 1 - 2 * core)
    n_chip = SIDE * SIDE
    rows = PER * HEAD
    piece = rows // n_chip
    hw = HEAD // 2

    def plane(dx, dy):
        o = lax.rem(cx + dx, SIDE) * SIDE + lax.rem(cy + dy, SIDE)
        return o, (dp, o * 2 + core)

    def zline(d):
        return (lax.rem(dp + d, n_dp), ctx)

    def remote(src, dst, ssem, rsem, where):
        return pltpu.make_async_remote_copy(
            src_ref=src, dst_ref=dst, send_sem=ssem, recv_sem=rsem,
            device_id=where, device_id_type=MESH,
        )

    def bulk(buf, ssem, rsem):
        return remote(buf, buf, ssem, rsem, near)

    def head(c, g, i):
        n = 2 * c + i
        return SIDE * n + lax.rem(n + g, SIDE)

    def cols(h):
        return pl.ds(pl.multiple_of(h * HEAD, HEAD), HEAD)

    def place(g, i):
        return pl.ds((g * PER + i) * HEAD, HEAD)

    w_load = pltpu.make_async_copy(w_hbm, w_ref, w_sem)
    loads = [
        pltpu.make_async_copy(src.at[0], raw.at[a], in_sem.at[a])
        for a, src in ((K, k_hbm), (V, v_hbm), (Q, q_hbm), (G, g_hbm))
    ]
    loads[K].start()
    loads[V].start()
    w_load.start()

    barrier = pltpu.get_barrier_semaphore()

    def greet(sem, where):
        pl.semaphore_signal(sem, inc=1, device_id=where, device_id_type=MESH)

    for d in FAR_FIRST:
        greet(barrier, plane(*d)[1])
    greet(barrier, near)
    greet(barrier, zline(1))
    greet(barrier, zline(n_dp - 1))

    def enter():
        loads[Q].start()
        loads[G].start()
        pl.semaphore_wait(barrier, 1 + len(FAR_FIRST) + 2)
        greet(near_sem, zline(1))
        greet(near_sem, zline(n_dp - 1))

    def relay():
        pl.semaphore_wait(near_sem, 2)
        greet(far_sem, zline(2))
        greet(far_sem, zline(n_dp - 2))

    def relayed():
        pl.semaphore_wait(far_sem, 2)

    rowid = lax.broadcasted_iota(jnp.int32, (tok, tok), 0)
    colid = lax.broadcasted_iota(jnp.int32, (tok, tok), 1)
    causal = rowid >= colid
    causal_t = rowid <= colid

    def lockstep(g, body):
        running = [body(g, i, b) for i in range(PER) for b in range(2)]
        while running:
            alive = []
            for r in running:
                try:
                    next(r)
                    alive.append(r)
                except StopIteration:
                    pass
            running = alive

    def pack(a, g):
        for i in range(PER):
            give[a, g, i] = raw[a, :, cols(head(1 - core, g, i))].astype(F32)
        remote(give.at[a, g], got.at[a, g], s_in.at[a, g], r_in.at[a, g], near).start()

    def keep(a, g):
        for i in range(PER):
            loc[a, 0, :, place(g, i)] = raw[a, :, cols(head(core, g, i))]

    def unpack(a, g):
        bulk(got.at[a, g], s_in.at[a, g], r_in.at[a, g]).wait_recv()
        for i in range(PER):
            loc[a, 1, :, place(g, i)] = got[a, g, i].astype(BF)

    def emit(o, g, i, b, value):
        if b == 0:
            res[o, :, cols(head(core, g, i))] = value.astype(BF)
        else:
            back[o, g, i] = value

    def send_back(o, g):
        remote(back.at[o, g], came.at[o, g], s_back.at[o, g], r_back.at[o, g], near).start()

    def take_back(o, g):
        bulk(came.at[o, g], s_back.at[o, g], r_back.at[o, g]).wait_recv()
        for i in range(PER):
            res[o, :, cols(head(1 - core, g, i))] = came[o, g, i].astype(BF)

    def weight(g, i):
        return w_ref[cols(head(core, g, i)), :]

    def outside(e, g, i, b):
        use = (core == 1) if e == b else (core == 0)
        other = state[e, 1 - b, place(g, i), :]
        return ret[e, g, pl.ds(i * HEAD, HEAD), :] + jnp.where(use, other, 0.0)

    def forward_state(g, i, b):
        c = place(g, i)
        z = dot(loc[K, b, :, c], weight(g, i), 1, 0)
        yield
        f = phi(z)
        kf = f.astype(BF)
        kf_ref[b, :, c] = kf
        sk_ref[b, :, c] = jnp.minimum(f, 1.0)
        yield
        state[0, b, c, :] = dot(kf, loc[V, b, :, c], 0, 0)

    def forward_local(g, i, b):
        c = place(g, i)
        z = dot(loc[Q, b, :, c], weight(g, i), 1, 0)
        yield
        f = phi(z)
        qf = f.astype(BF)
        qf_ref[b, :, c] = qf
        sq_ref[b, :, c] = jnp.minimum(f, 1.0)
        yield
        kf = kf_ref[b, :, c]
        w = jnp.where(causal, dot(qf, kf, 1, 1), 0.0).astype(BF)
        sct_ref[b, :, c] = jnp.where(causal_t, dot(kf, qf, 1, 1), 0.0).astype(BF)
        yield
        nl_ref[b, :, c] = dot(w, loc[V, b, :, c], 1, 0)

    def numer(g, i, b):
        c = place(g, i)
        qf = qf_ref[b, :, c]
        ph, plo = split(outside(0, g, i, b))
        yield
        n = dot(qf, ph, 1, 0) + dot(qf, plo, 1, 0) + nl_ref[b, :, c]
        yield
        r = lax.rsqrt(jnp.mean(n * n, axis=-1, keepdims=True) + EPS)
        yield
        normed = n * r
        og = loc[G, b, :, c].astype(F32)
        s = jnp.mean(og * normed, axis=-1, keepdims=True)
        yield
        m = (r * (og - normed * s)).astype(BF)
        m_ref[b, :, c] = m
        yield
        state[1, b, c, :] = dot(qf, m, 0, 0)
        emit(ATT, g, i, b, normed)

    def back_local(g, i, b):
        c = place(g, i)
        m, qf, kf, v = m_ref[b, :, c], qf_ref[b, :, c], kf_ref[b, :, c], loc[V, b, :, c]
        ph, plo = split(outside(0, g, i, b))
        s = jnp.where(causal, dot(m, v, 1, 1), 0.0).astype(BF)
        st = jnp.where(causal_t, dot(v, m, 1, 1), 0.0).astype(BF)
        yield
        qg = dot(m, ph, 1, 1) + dot(m, plo, 1, 1) + dot(s, kf, 1, 0)
        dkl_ref[b, :, c] = dot(st, qf, 1, 0)
        dvl_ref[b, :, c] = dot(sct_ref[b, :, c], m, 1, 0)
        yield
        qp = (qg * sq_ref[b, :, c]).astype(BF)
        yield
        wl_ref[b, c, :] = dot(loc[Q, b, :, c], qp, 0, 0)
        emit(DQ, g, i, b, dot(qp, weight(g, i), 1, 1))

    def back_final(g, i, b):
        c = place(g, i)
        qh, ql = split(outside(1, g, i, b))
        v, kf = loc[V, b, :, c], kf_ref[b, :, c]
        yield
        kg = dot(v, qh, 1, 1) + dot(v, ql, 1, 1) + dkl_ref[b, :, c]
        yield
        kp = (kg * sk_ref[b, :, c]).astype(BF)
        yield
        wl_ref[b, c, :] += dot(loc[K, b, :, c], kp, 0, 0)
        yield
        dv = dot(kf, qh, 1, 0) + dot(kf, ql, 1, 0) + dvl_ref[b, :, c]
        dk = dot(kp, weight(g, i), 1, 1)
        yield
        emit(DV, g, i, b, dv)
        emit(DK, g, i, b, dk)

    def part(o):
        return pl.ds(pl.multiple_of(o * piece, piece), piece)

    def scan_gather(e, g):
        c = pl.ds(g * rows, rows)
        pair[e, g] = state[e, 0, c, :] + state[e, 1, c, :]
        for d in FAR_FIRST:
            o, where = plane(*d)
            remote(
                pair.at[e, g, part(o), :], gat.at[e, g, chip],
                s_gat.at[e, g], r_gat.at[e, g], where,
            ).start()
        gat[e, g, chip] = pair[e, g, part(chip), :]

    def scan_return(e, g):
        bulk(gat.at[e, g, pl.ds(0, n_chip - 1)], s_gat.at[e, g], r_gat.at[e, g]).wait_recv()
        order = range(n_chip) if e == 0 else range(n_chip - 1, -1, -1)
        total = jnp.zeros((piece, HEAD), F32)
        for p in order:
            pre[e, g, p] = total
            total = total + gat[e, g, p]
        for d in FAR_FIRST:
            o, where = plane(*d)
            remote(
                pre.at[e, g, o], ret.at[e, g, part(chip), :],
                s_ret.at[e, g], r_ret.at[e, g], where,
            ).start()
        ret[e, g, part(chip), :] = pre[e, g, chip]

    def scan_wait(e, g):
        bulk(
            ret.at[e, g, pl.ds(0, rows - piece), :], s_ret.at[e, g], r_ret.at[e, g]
        ).wait_recv()

    def weight_parts(g):
        for i in range(PER):
            h = head(core, g, i)
            for c in range(2):
                yield i, c, (dp, 2 * h + c), (chip == h) & (core == c)

    def weight_send(g):
        for i in range(PER):
            wl_ref[0, place(g, i), :] += wl_ref[1, place(g, i), :]
        for i, c, where, own in weight_parts(g):
            part_rows = pl.ds((g * PER + i) * HEAD + c * hw, hw)

            @pl.when(jnp.logical_not(own))
            def _():
                remote(
                    wl_ref.at[0, part_rows, :], wgat.at[chip], s_wg.at[g, i, c], r_wg, where
                ).start()

            @pl.when(own)
            def _():
                wgat[chip] = wl_ref[0, part_rows, :]

    def weight_sum():
        own = core == lax.div(chip, n_chip // 2)

        @pl.when(own)
        def _():
            bulk(wgat.at[pl.ds(0, n_chip - 1)], s_z, r_wg).wait_recv()

        @pl.when(jnp.logical_not(own))
        def _():
            bulk(wgat, s_z, r_wg).wait_recv()

        total = wgat[0]
        for p in range(1, n_chip):
            total = total + wgat[p]
        zsrc[...] = total
        for d in (4, 3, 5, 2, 6, 1, 7):
            remote(zsrc, zgat.at[dp], s_z, r_z, zline(d)).start()
        zgat[dp] = total

    def weight_finish():
        bulk(zgat.at[pl.ds(0, n_dp - 1)], s_z, r_z).wait_recv()
        total = zgat[0]
        for z in range(1, n_dp):
            total = total + zgat[z]
        wg_ref[...] = total

    stores = []

    def store(o, dst):
        c = pltpu.make_async_copy(res.at[o], dst.at[0], out_sem.at[o])
        c.start()
        stores.append(c)

    first = [False] * 3

    def once(i, action):
        if not first[i]:
            first[i] = True
            action()

    def step(name, g):
        if name == "pk":
            once(0, lambda: (loads[K].wait(), loads[V].wait(), enter()))
            pack(K, g)
            pack(V, g)
        elif name == "fs":
            once(1, lambda: w_load.wait())
            keep(K, g)
            keep(V, g)
            unpack(K, g)
            unpack(V, g)
            lockstep(g, forward_state)
            scan_gather(0, g)
        elif name == "pq":
            once(2, lambda: (loads[Q].wait(), loads[G].wait()))
            pack(Q, g)
            pack(G, g)
            keep(Q, g)
            keep(G, g)
        elif name == "fl":
            unpack(Q, g)
            unpack(G, g)
            lockstep(g, forward_local)
        elif name == "c0":
            scan_return(0, g)
        elif name == "nu":
            scan_wait(0, g)
            lockstep(g, numer)
            scan_gather(1, g)
            send_back(ATT, g)
        elif name == "bl":
            lockstep(g, back_local)
            send_back(DQ, g)
        elif name == "c1":
            scan_return(1, g)
        elif name == "bf":
            scan_wait(1, g)
            lockstep(g, back_final)
            weight_send(g)
            send_back(DK, g)
            send_back(DV, g)

    for word in ORDER:
        if word == "relay":
            relay()
        elif word == "relayed":
            relayed()
        else:
            step(word[:-1], int(word[-1]))
    for g in range(GROUPS):
        take_back(ATT, g)
        take_back(DQ, g)
    store(ATT, att_hbm)
    store(DQ, dq_hbm)
    weight_sum()
    for g in range(GROUPS):
        take_back(DK, g)
        take_back(DV, g)
    store(DK, dk_hbm)
    store(DV, dv_hbm)
    weight_finish()
    wg_out = pltpu.make_async_copy(wg_ref, wg_hbm, w_sem)
    wg_out.start()

    for g in range(GROUPS):
        for a in range(4):
            bulk(give.at[a, g], s_in.at[a, g], r_in.at[a, g]).wait_send()
            bulk(back.at[a, g], s_back.at[a, g], r_back.at[a, g]).wait_send()
        for e in range(2):
            bulk(gat.at[e, g, pl.ds(0, n_chip - 1)], s_gat.at[e, g], r_gat.at[e, g]).wait_send()
            bulk(pre.at[e, g, pl.ds(0, n_chip - 1)], s_ret.at[e, g], r_ret.at[e, g]).wait_send()
        for i, c, where, own in weight_parts(g):

            @pl.when(jnp.logical_not(own))
            def _():
                bulk(zsrc, s_wg.at[g, i, c], r_wg).wait_send()

    bulk(zgat.at[pl.ds(0, n_dp - 1)], s_z, r_z).wait_send()
    for c in stores:
        c.wait()
    wg_out.wait()


def body(n_dp, q, k, v, g, w):
    _, tok, width = q.shape
    mine = GROUPS * PER * HEAD
    rows = PER * HEAD
    n_chip = SIDE * SIDE
    hw = HEAD // 2
    dma = pltpu.SemaphoreType.DMA
    act = pltpu.VMEM((2, tok, mine), BF)
    wide = pltpu.VMEM((2, tok, mine), F32)
    moved = pltpu.VMEM((4, GROUPS, PER, tok, HEAD), F32)
    block = pltpu.VMEM((2, GROUPS, rows, HEAD), F32)
    slots = pltpu.VMEM((2, GROUPS, n_chip, rows // n_chip, HEAD), F32)
    part = pltpu.VMEM((hw, HEAD), F32)
    scratch = (
        [pltpu.VMEM((4, tok, width), BF), pltpu.VMEM((width, HEAD), BF)]
        + [pltpu.VMEM((4, tok, width), BF), part]
        + [pltpu.VMEM((4, 2, tok, mine), BF)] + [moved] * 4
        + [act] * 4 + [wide] * 5
        + [pltpu.VMEM((2, 2, mine, HEAD), F32), block, slots, slots, block]
        + [pltpu.VMEM((2, mine, HEAD), F32), pltpu.VMEM((n_chip, hw, HEAD), F32)]
        + [part, pltpu.VMEM((n_dp, hw, HEAD), F32)]
        + [dma((4,)), dma, dma((4,))]
        + [dma((4, GROUPS))] * 4 + [dma((2, GROUPS))] * 4
        + [dma((GROUPS, PER, 2)), dma, dma, dma]
        + [pltpu.SemaphoreType.REGULAR] * 2
    )
    outs = [jax.ShapeDtypeStruct(q.shape, BF)] * 4 + [jax.ShapeDtypeStruct((hw, HEAD), F32)]
    hbm = pl.BlockSpec(memory_space=pl.ANY)
    limit = 63 * 1024 * 1024
    results = pl.pallas_call(
        functools.partial(kernel, n_dp, tok),
        out_shape=outs,
        in_specs=[hbm] * 5,
        out_specs=[hbm] * 5,
        scratch_shapes=scratch,
        compiler_params=pltpu.CompilerParams(
            collective_id=0, has_side_effects=True, vmem_limit_bytes=limit
        ),
        cost_estimate=pl.CostEstimate(
            flops=80 * mine * HEAD**2, bytes_accessed=5 * 2**20, transcendentals=0
        ),
    )(q, k, v, g, w)
    return pl.pallas_call(
        write_out,
        out_shape=outs,
        in_specs=[hbm] * 5,
        out_specs=[hbm] * 5,
        scratch_shapes=[pltpu.VMEM(o.shape, o.dtype) for o in outs] + [dma((2, 5))],
        compiler_params=pltpu.CompilerParams(vmem_limit_bytes=limit),
    )(*results)


def solution(mesh):
    spec = P("dp", "ctx", None)
    return jax.shard_map(
        functools.partial(body, mesh.shape["dp"]),
        mesh=mesh,
        in_specs=(spec, spec, spec, spec, P()),
        out_specs=(spec, spec, spec, spec, P("ctx", None)),
        check_vma=False,
    )
```

time: 63.2 us -> 59 us (0.934)
  Pallas kernels: 62.3 us -> 58.2 us
    pallas_call x1, Pallas kernels: 59.9 us -> 55.8 us  [body(): pl.pallas_call(functools.partial(kernel, n_dp, tok), out_shape=outs, in_s...]
where the time goes in v3:
time: 59 us; the launch traced here: 58.9 us
  Pallas kernels  58.2 us (99%)
  between operations  0.64 us (1%)
    pallas_call x1, Pallas kernels, body(): pl.pallas_call(functools.partial(kernel, n_dp, tok), out_shape=outs, in_s...  55.8 us
    pallas_call x1, Pallas kernels, body(): pl.pallas_call(write_out, out_shape=outs, in_specs=[hbm] * 5, out_specs=[...  2.44 us

profile of v3, /device:TPU:2, one launch (start us, length us, event | category | flops | bytes accessed | tf_op | source)
XLA Modules:
  0.0 58.9 jit_solution(15132003070511961629)
XLA Ops:
  0.6 55.8 %shard_map.92 = (bf16[1,128,2048]{2,1,0:T(8,128)(2,1)}, bf16[1,128,2048]{2,1,0:T(8,128)(2,1)}, bf16[1,128,2048]{2,1,0:T(8,128)(2,1)}, bf16[1,128,2048]{2,1,0:T(8,128)(2,1)}, f32[64,128]{1,0:T(8,128)}) custom-call(bf16[1,128,2048]{2,1,0:T(8,128)(2,1)} %q_hbm.1, bf16[1,128,2048]{2,1,0:T(8,128)(2,1)} %k_hbm.1, bf16[1,128,2048]{2,1,0:T(8,128)(2,1)} %v_hbm.1, ...), custom_call_target="tpu_custom_call" | custom-call | flops 1342177280 | bytes 5242880 | tf_op jit(solution)/shard_map/pallas_call | solution.py:482
  56.4 2.4 %shard_map.93 = (bf16[1,128,2048]{2,1,0:T(8,128)(2,1)}, bf16[1,128,2048]{2,1,0:T(8,128)(2,1)}, bf16[1,128,2048]{2,1,0:T(8,128)(2,1)}, bf16[1,128,2048]{2,1,0:T(8,128)(2,1)}, f32[64,128]{1,0:T(8,128)}) custom-call(bf16[1,128,2048]{2,1,0:T(8,128)(2,1)} %get-tuple-element.10.refs_0_, bf16[1,128,2048]{2,1,0:T(8,128)(2,1)} %get-tuple-element.11.refs_1_, ...), custom_call_target="tpu_custom_call" | custom-call | tf_op jit(solution)/shard_map/pallas_call | solution.py:495

commit v4 on v3

--- a/solution.py
+++ b/solution.py
@@ -9,10 +9,10 @@
 
 HEAD = 128
 ORDER = (
-    "pk0", "pk1", "fs0", "pk2", "fs1", "pk3", "fs2", "fs3", "pq0", "pq1", "pq2", "pq3", "fl0",
-    "fl1", "c00", "c01", "fl2", "c02", "fl3", "c03", "relay", "nu0", "nu1", "nu2", "nu3",
-    "relayed", "bl0", "bl1", "c10", "bl2", "c11", "bl3", "c12", "c13", "bf0", "bf1", "bf2",
-    "bf3",
+    "fs0", "fs1", "fs2", "fs3", "ss0", "ss1", "ss2", "ss3", "gs0", "gs1", "gs2", "gs3", "pk0",
+    "pk1", "pq0", "pq1", "pk2", "pk3", "pq2", "pq3", "kf0", "fl0", "kf1", "fl1", "c00", "c01",
+    "kf2", "fl2", "c02", "kf3", "fl3", "c03", "relay", "nu0", "nu1", "nu2", "nu3", "relayed",
+    "bl0", "bl1", "c10", "bl2", "c11", "bl3", "c12", "c13", "bf0", "bf1", "bf2", "bf3",
 )
 EPS = 1e-05
 SIDE = 4
@@ -62,11 +62,11 @@
     raw, w_ref, res, wg_ref,
     loc, give, got, back, came,
     qf_ref, kf_ref, sct_ref, m_ref, sq_ref, sk_ref, nl_ref, dkl_ref, dvl_ref,
-    state, pair, gat, pre, ret,
+    state, lent, pair, gat, pre, ret,
     wl_ref, wgat, zsrc, zgat,
     in_sem, w_sem, out_sem,
     s_in, r_in, s_back, r_back, s_gat, r_gat, s_ret, r_ret,
-    s_wg, r_wg, s_z, r_z, near_sem, far_sem,
+    s_lent, r_lent, s_wg, r_wg, s_z, r_z, near_sem, far_sem,
 ):
     dp = lax.axis_index("dp")
     ctx = lax.axis_index("ctx")
@@ -145,8 +145,8 @@
     causal = rowid >= colid
     causal_t = rowid <= colid
 
-    def lockstep(g, body):
-        running = [body(g, i, b) for i in range(PER) for b in range(2)]
+    def lockstep(g, body, blocks=(0, 1)):
+        running = [body(g, i, b) for i in range(PER) for b in blocks]
         while running:
             alive = []
             for r in running:
@@ -193,16 +193,34 @@
         other = state[e, 1 - b, place(g, i), :]
         return ret[e, g, pl.ds(i * HEAD, HEAD), :] + jnp.where(use, other, 0.0)
 
-    def forward_state(g, i, b):
+    def key_side(g, i, b):
         c = place(g, i)
         z = dot(loc[K, b, :, c], weight(g, i), 1, 0)
         yield
         f = phi(z)
+        kf_ref[b, :, c] = f.astype(BF)
+        sk_ref[b, :, c] = jnp.minimum(f, 1.0)
+
+    def forward_state(g, i, own):
+        c = cols(head(core if own else 1 - core, g, i))
+        z = dot(raw[K, :, c], w_ref[c, :], 1, 0)
+        yield
+        f = phi(z)
         kf = f.astype(BF)
-        kf_ref[b, :, c] = kf
-        sk_ref[b, :, c] = jnp.minimum(f, 1.0)
-        yield
-        state[0, b, c, :] = dot(kf, loc[V, b, :, c], 0, 0)
+        if own:
+            kf_ref[0, :, place(g, i)] = kf
+            sk_ref[0, :, place(g, i)] = jnp.minimum(f, 1.0)
+        yield
+        s = dot(kf, raw[V, :, c], 0, 0)
+        if own:
+            state[0, 0, place(g, i), :] = s
+        else:
+            lent[g, pl.ds(i * HEAD, HEAD), :] = s
+
+    def swap_state(g):
+        return remote(
+            lent.at[g], state.at[0, 1, pl.ds(g * rows, rows), :], s_lent.at[g], r_lent.at[g], near
+        )
 
     def forward_local(g, i, b):
         c = place(g, i)
@@ -342,8 +360,12 @@
         for p in range(1, n_chip):
             total = total + wgat[p]
         zsrc[...] = total
-        for d in (4, 3, 5, 2, 6, 1, 7):
-            remote(zsrc, zgat.at[dp], s_z, r_z, zline(d)).start()
+        for z in range(n_dp):
+
+            @pl.when(z != dp)
+            def _():
+                remote(zsrc, zgat.at[dp], s_z, r_z, (z, ctx)).start()
+
         zgat[dp] = total
 
     def weight_finish():
@@ -368,24 +390,30 @@
             action()
 
     def step(name, g):
-        if name == "pk":
-            once(0, lambda: (loads[K].wait(), loads[V].wait(), enter()))
+        if name == "fs":
+            once(0, lambda: (loads[K].wait(), loads[V].wait(), w_load.wait()))
+            lockstep(g, forward_state, (True, False))
+        elif name == "ss":
+            once(1, enter)
+            swap_state(g).start()
+        elif name == "gs":
+            swap_state(g).wait_recv()
+            scan_gather(0, g)
+        elif name == "pk":
             pack(K, g)
             pack(V, g)
-        elif name == "fs":
-            once(1, lambda: w_load.wait())
             keep(K, g)
             keep(V, g)
-            unpack(K, g)
-            unpack(V, g)
-            lockstep(g, forward_state)
-            scan_gather(0, g)
         elif name == "pq":
             once(2, lambda: (loads[Q].wait(), loads[G].wait()))
             pack(Q, g)
             pack(G, g)
             keep(Q, g)
             keep(G, g)
+        elif name == "kf":
+            unpack(K, g)
+            unpack(V, g)
+            lockstep(g, key_side, (1,))
         elif name == "fl":
             unpack(Q, g)
             unpack(G, g)
@@ -432,6 +460,7 @@
     wg_out.start()
 
     for g in range(GROUPS):
+        swap_state(g).wait_send()
         for a in range(4):
             bulk(give.at[a, g], s_in.at[a, g], r_in.at[a, g]).wait_send()
             bulk(back.at[a, g], s_back.at[a, g], r_back.at[a, g]).wait_send()
@@ -468,12 +497,12 @@
         + [pltpu.VMEM((4, tok, width), BF), part]
         + [pltpu.VMEM((4, 2, tok, mine), BF)] + [moved] * 4
         + [act] * 4 + [wide] * 5
-        + [pltpu.VMEM((2, 2, mine, HEAD), F32), block, slots, slots, block]
+        + [pltpu.VMEM((2, 2, mine, HEAD), F32), pltpu.VMEM((GROUPS, rows, HEAD), F32), block, slots, slots, block]
         + [pltpu.VMEM((2, mine, HEAD), F32), pltpu.VMEM((n_chip, hw, HEAD), F32)]
         + [part, pltpu.VMEM((n_dp, hw, HEAD), F32)]
         + [dma((4,)), dma, dma((4,))]
         + [dma((4, GROUPS))] * 4 + [dma((2, GROUPS))] * 4
-        + [dma((GROUPS, PER, 2)), dma, dma, dma]
+        + [dma((GROUPS,))] * 2 + [dma((GROUPS, PER, 2)), dma, dma, dma]
         + [pltpu.SemaphoreType.REGULAR] * 2
     )
     outs = [jax.ShapeDtypeStruct(q.shape, BF)] * 4 + [jax.ShapeDtypeStruct((hw, HEAD), F32)]

time: 59 us -> 57.8 us (0.980)
  Pallas kernels: 58.2 us -> 56.5 us
    pallas_call x1, Pallas kernels: 55.8 us -> 54 us  [body(): pl.pallas_call(functools.partial(kernel, n_dp, tok), out_shape=outs, in_s...]
where the time goes in v4:
time: 57.8 us; the launch traced here: 57.1 us
  Pallas kernels  56.5 us (98%)
  between operations  0.64 us (1%)
    pallas_call x1, Pallas kernels, body(): pl.pallas_call(functools.partial(kernel, n_dp, tok), out_shape=outs, in_s...  54 us
    pallas_call x1, Pallas kernels, body(): pl.pallas_call(write_out, out_shape=outs, in_specs=[hbm] * 5, out_specs=[...  2.44 us

profile of v4, /device:TPU:2, one launch (start us, length us, event | category | flops | bytes accessed | tf_op | source)
XLA Modules:
  0.0 57.1 jit_solution(5315946037229166024)
XLA Ops:
  0.6 54.0 %shard_map.92 = (bf16[1,128,2048]{2,1,0:T(8,128)(2,1)}, bf16[1,128,2048]{2,1,0:T(8,128)(2,1)}, bf16[1,128,2048]{2,1,0:T(8,128)(2,1)}, bf16[1,128,2048]{2,1,0:T(8,128)(2,1)}, f32[64,128]{1,0:T(8,128)}) custom-call(bf16[1,128,2048]{2,1,0:T(8,128)(2,1)} %q_hbm.1, bf16[1,128,2048]{2,1,0:T(8,128)(2,1)} %k_hbm.1, bf16[1,128,2048]{2,1,0:T(8,128)(2,1)} %v_hbm.1, ...), custom_call_target="tpu_custom_call" | custom-call | flops 1342177280 | bytes 5242880 | tf_op jit(solution)/shard_map/pallas_call | solution.py:511
  54.6 2.4 %shard_map.93 = (bf16[1,128,2048]{2,1,0:T(8,128)(2,1)}, bf16[1,128,2048]{2,1,0:T(8,128)(2,1)}, bf16[1,128,2048]{2,1,0:T(8,128)(2,1)}, bf16[1,128,2048]{2,1,0:T(8,128)(2,1)}, f32[64,128]{1,0:T(8,128)}) custom-call(bf16[1,128,2048]{2,1,0:T(8,128)(2,1)} %get-tuple-element.10.refs_0_, bf16[1,128,2048]{2,1,0:T(8,128)(2,1)} %get-tuple-element.11.refs_1_, ...), custom_call_target="tpu_custom_call" | custom-call | tf_op jit(solution)/shard_map/pallas_call | solution.py:524

commit v5 on v4

--- a/solution.py
+++ b/solution.py
@@ -10,9 +10,10 @@
 HEAD = 128
 ORDER = (
     "fs0", "fs1", "fs2", "fs3", "ss0", "ss1", "ss2", "ss3", "gs0", "gs1", "gs2", "gs3", "pk0",
-    "pk1", "pq0", "pq1", "pk2", "pk3", "pq2", "pq3", "kf0", "fl0", "kf1", "fl1", "c00", "c01",
-    "kf2", "fl2", "c02", "kf3", "fl3", "c03", "relay", "nu0", "nu1", "nu2", "nu3", "relayed",
-    "bl0", "bl1", "c10", "bl2", "c11", "bl3", "c12", "c13", "bf0", "bf1", "bf2", "bf3",
+    "pk1", "pq0", "pq1", "pk2", "pk3", "pq2", "pq3", "kf0", "fl0", "kf1", "c00", "fl1", "c01",
+    "kf2", "c02", "fl2", "c03", "kf3", "fl3", "relay", "nu0", "nu1", "nu2", "nu3", "relayed",
+    "bl0", "c10", "bl1", "c11", "bl2", "c12", "bl3", "c13", "bf0", "bf1", "bf2", "bf3", "br0",
+    "br1", "br2", "br3",
 )
 EPS = 1e-05
 SIDE = 4
@@ -61,7 +62,7 @@
     att_hbm, dq_hbm, dk_hbm, dv_hbm, wg_hbm,
     raw, w_ref, res, wg_ref,
     loc, give, got, back, came,
-    qf_ref, kf_ref, sct_ref, m_ref, sq_ref, sk_ref, nl_ref, dkl_ref, dvl_ref,
+    qf_ref, kf_ref, sct_ref, m_ref, kp_ref, sq_ref, sk_ref, nl_ref, dkl_ref, dvl_ref,
     state, lent, pair, gat, pre, ret,
     wl_ref, wgat, zsrc, zgat,
     in_sem, w_sem, out_sem,
@@ -275,16 +276,22 @@
     def back_final(g, i, b):
         c = place(g, i)
         qh, ql = split(outside(1, g, i, b))
-        v, kf = loc[V, b, :, c], kf_ref[b, :, c]
+        v = loc[V, b, :, c]
         yield
         kg = dot(v, qh, 1, 1) + dot(v, ql, 1, 1) + dkl_ref[b, :, c]
         yield
         kp = (kg * sk_ref[b, :, c]).astype(BF)
+        kp_ref[b, :, c] = kp
         yield
         wl_ref[b, c, :] += dot(loc[K, b, :, c], kp, 0, 0)
+
+    def back_rest(g, i, b):
+        c = place(g, i)
+        qh, ql = split(outside(1, g, i, b))
+        kf = kf_ref[b, :, c]
         yield
         dv = dot(kf, qh, 1, 0) + dot(kf, ql, 1, 0) + dvl_ref[b, :, c]
-        dk = dot(kp, weight(g, i), 1, 1)
+        dk = dot(kp_ref[b, :, c], weight(g, i), 1, 1)
         yield
         emit(DV, g, i, b, dv)
         emit(DK, g, i, b, dk)
@@ -434,6 +441,8 @@
             scan_wait(1, g)
             lockstep(g, back_final)
             weight_send(g)
+        elif name == "br":
+            lockstep(g, back_rest)
             send_back(DK, g)
             send_back(DV, g)
 
@@ -444,12 +453,12 @@
             relayed()
         else:
             step(word[:-1], int(word[-1]))
+    weight_sum()
     for g in range(GROUPS):
         take_back(ATT, g)
         take_back(DQ, g)
     store(ATT, att_hbm)
     store(DQ, dq_hbm)
-    weight_sum()
     for g in range(GROUPS):
         take_back(DK, g)
         take_back(DV, g)
@@ -496,7 +505,7 @@
         [pltpu.VMEM((4, tok, width), BF), pltpu.VMEM((width, HEAD), BF)]
         + [pltpu.VMEM((4, tok, width), BF), part]
         + [pltpu.VMEM((4, 2, tok, mine), BF)] + [moved] * 4
-        + [act] * 4 + [wide] * 5
+        + [act] * 5 + [wide] * 5
         + [pltpu.VMEM((2, 2, mine, HEAD), F32), pltpu.VMEM((GROUPS, rows, HEAD), F32), block, slots, slots, block]
         + [pltpu.VMEM((2, mine, HEAD), F32), pltpu.VMEM((n_chip, hw, HEAD), F32)]
         + [part, pltpu.VMEM((n_dp, hw, HEAD), F32)]

time: 57.8 us -> 57.5 us (level)
  no operation moved by 1% of the time
where the time goes in v5:
time: 57.5 us; the launch traced here: 56.9 us
  Pallas kernels  56.3 us (98%)
  between operations  0.64 us (1%)
    pallas_call x1, Pallas kernels, body(): pl.pallas_call(functools.partial(kernel, n_dp, tok), out_shape=outs, in_s...  53.9 us
    pallas_call x1, Pallas kernels, body(): pl.pallas_call(write_out, out_shape=outs, in_specs=[hbm] * 5, out_specs=[...  2.44 us

profile of v5, /device:TPU:2, one launch (start us, length us, event | category | flops | bytes accessed | tf_op | source)
XLA Modules:
  0.0 56.9 jit_solution(501356596616238444)
XLA Ops:
  0.6 53.9 %shard_map.92 = (bf16[1,128,2048]{2,1,0:T(8,128)(2,1)}, bf16[1,128,2048]{2,1,0:T(8,128)(2,1)}, bf16[1,128,2048]{2,1,0:T(8,128)(2,1)}, bf16[1,128,2048]{2,1,0:T(8,128)(2,1)}, f32[64,128]{1,0:T(8,128)}) custom-call(bf16[1,128,2048]{2,1,0:T(8,128)(2,1)} %q_hbm.1, bf16[1,128,2048]{2,1,0:T(8,128)(2,1)} %k_hbm.1, bf16[1,128,2048]{2,1,0:T(8,128)(2,1)} %v_hbm.1, ...), custom_call_target="tpu_custom_call" | custom-call | flops 1342177280 | bytes 5242880 | tf_op jit(solution)/shard_map/pallas_call | solution.py:520
  54.5 2.4 %shard_map.93 = (bf16[1,128,2048]{2,1,0:T(8,128)(2,1)}, bf16[1,128,2048]{2,1,0:T(8,128)(2,1)}, bf16[1,128,2048]{2,1,0:T(8,128)(2,1)}, bf16[1,128,2048]{2,1,0:T(8,128)(2,1)}, f32[64,128]{1,0:T(8,128)}) custom-call(bf16[1,128,2048]{2,1,0:T(8,128)(2,1)} %get-tuple-element.10.refs_0_, bf16[1,128,2048]{2,1,0:T(8,128)(2,1)} %get-tuple-element.11.refs_1_, ...), custom_call_target="tpu_custom_call" | custom-call | tf_op jit(solution)/shard_map/pallas_call | solution.py:533

commit v6 on v5

--- a/solution.py
+++ b/solution.py
@@ -248,6 +248,7 @@
         r = lax.rsqrt(jnp.mean(n * n, axis=-1, keepdims=True) + EPS)
         yield
         normed = n * r
+        nl_ref[b, :, c] = normed
         og = loc[G, b, :, c].astype(F32)
         s = jnp.mean(og * normed, axis=-1, keepdims=True)
         yield
@@ -255,7 +256,10 @@
         m_ref[b, :, c] = m
         yield
         state[1, b, c, :] = dot(qf, m, 0, 0)
-        emit(ATT, g, i, b, normed)
+
+    def attend(g, i, b):
+        emit(ATT, g, i, b, nl_ref[b, :, place(g, i)])
+        yield
 
     def back_local(g, i, b):
         c = place(g, i)
@@ -431,6 +435,7 @@
             scan_wait(0, g)
             lockstep(g, numer)
             scan_gather(1, g)
+            lockstep(g, attend)
             send_back(ATT, g)
         elif name == "bl":
             lockstep(g, back_local)

time: 57.5 us -> 57.5 us (level)
  no operation moved by 1% of the time
where the time goes in v6:
time: 57.5 us; the launch traced here: 56.9 us
  Pallas kernels  56.3 us (98%)
  between operations  0.64 us (1%)
    pallas_call x1, Pallas kernels, body(): pl.pallas_call(functools.partial(kernel, n_dp, tok), out_shape=outs, in_s...  53.9 us
    pallas_call x1, Pallas kernels, body(): pl.pallas_call(write_out, out_shape=outs, in_specs=[hbm] * 5, out_specs=[...  2.44 us

profile of v6, /device:TPU:2, one launch (start us, length us, event | category | flops | bytes accessed | tf_op | source)
XLA Modules:
  0.0 56.9 jit_solution(1660210905549809076)
XLA Ops:
  0.6 53.9 %shard_map.92 = (bf16[1,128,2048]{2,1,0:T(8,128)(2,1)}, bf16[1,128,2048]{2,1,0:T(8,128)(2,1)}, bf16[1,128,2048]{2,1,0:T(8,128)(2,1)}, bf16[1,128,2048]{2,1,0:T(8,128)(2,1)}, f32[64,128]{1,0:T(8,128)}) custom-call(bf16[1,128,2048]{2,1,0:T(8,128)(2,1)} %q_hbm.1, bf16[1,128,2048]{2,1,0:T(8,128)(2,1)} %k_hbm.1, bf16[1,128,2048]{2,1,0:T(8,128)(2,1)} %v_hbm.1, ...), custom_call_target="tpu_custom_call" | custom-call | flops 1342177280 | bytes 5242880 | tf_op jit(solution)/shard_map/pallas_call | solution.py:525
  54.5 2.4 %shard_map.93 = (bf16[1,128,2048]{2,1,0:T(8,128)(2,1)}, bf16[1,128,2048]{2,1,0:T(8,128)(2,1)}, bf16[1,128,2048]{2,1,0:T(8,128)(2,1)}, bf16[1,128,2048]{2,1,0:T(8,128)(2,1)}, f32[64,128]{1,0:T(8,128)}) custom-call(bf16[1,128,2048]{2,1,0:T(8,128)(2,1)} %get-tuple-element.10.refs_0_, bf16[1,128,2048]{2,1,0:T(8,128)(2,1)} %get-tuple-element.11.refs_1_, ...), custom_call_target="tpu_custom_call" | custom-call | tf_op jit(solution)/shard_map/pallas_call | solution.py:538
